TPU v7x, 256 devices: a whole 4x4x8 slice. The times are simulated.
256 devices in a mesh: prow: 16 (over z_hi, y), pcol: 16 (over z_lo, x, core).
Axes of the slice: x: 4, y: 4, z: 8 (z_hi: 4, z_lo: 2; z = z_hi * 2 + z_lo), core: 2. Of those that a mesh axis runs over, the one named last changes fastest.
Arguments:
- top_inverse: float32 [8192, 8192], P('prow', 'pcol'), as said below
- panel_one: float32 [2560, 4096], P('prow', 'pcol'), may hold values from -0.125 to 0.125
- panel_two: float32 [1280, 8192], P('prow', 'pcol'), may hold values from -0.15625 to 0.15625
- parent_rows: float32 [256, 8192], P('prow', 'pcol'), may hold values from -0.15625 to 0.15625
- pivot_one: float32 [256, 4096], P('prow', 'pcol'), as said below
- pivot_two: float32 [256, 8192], P('prow', 'pcol'), as said below
- sets_one: int32 [16, 10], replicated, may hold values from 0 to 31, as said below
- sets_two: int32 [32, 5], replicated, may hold values from 0 to 31, as said below
Outputs:
- below_one: float32 [2560, 4096], P('prow', 'pcol')
- corner_one: float32 [256, 4096], P('prow', 'pcol')
- below_two: float32 [1280, 8192], P('prow', 'pcol')
- beside_two: float32 [256, 8192], P('prow', 'pcol')
- corner_two: float32 [256, 8192], P('prow', 'pcol')
Inputs may be any that keep to these rules, and one draw needn't show every extreme that they name: top_inverse is symmetric. `pivot_one`: every 256 x 256 column block is symmetric. `pivot_two`: every 256 x 256 column block is symmetric. `sets_one`: each row holds 10 different ancestor supernodes in increasing order. `sets_two`: row C holds 5 different entries of row C // 2 of sets_one, in increasing order.
All inputs are finite; a program needn't handle non-finite values.
Results may differ from a plain program's by a relative error of at most 0.0003.
Values sent between devices are 32-bit elements; how exact they have to be, the bound alone decides.
A program may use at most 128 MiB of HBM per device.

v0:
```python
import jax
import jax.numpy as jnp
from jax import lax
from jax.sharding import PartitionSpec as P

B = 256


EXACT = lax.Precision.HIGHEST


def column_index(sets):
    count = sets.shape[0]
    span = sets.shape[1]
    offsets = jnp.arange(B, dtype=jnp.int32)
    return (sets[:, :, None] * B + offsets[None, None, :]).reshape(count, span * B)


def placement(sets, first_block, block_rows):
    blocks = first_block + jnp.arange(block_rows, dtype=jnp.int32)
    return (sets[:, :, None] == blocks[None, None, :]).astype(jnp.float32)


def twice_each(values, rows, count):
    split = values.reshape(rows, count, 1, B)
    return jnp.broadcast_to(split, (rows, count, 2, B)).reshape(rows, 2 * count, B)


def fold_rows(total, piece, chosen):
    width = piece.shape[0]
    count = total.shape[1]
    return jnp.einsum("rjk,kje->rje", chosen, piece.reshape(width, count, B), precision=EXACT)


def on_device(
    top_inverse, panel_one, panel_two, parent_rows, pivot_one, pivot_two, sets_one, sets_two
):
    row_count = lax.axis_size("prow")
    row_index = lax.axis_index("prow")
    col_index = lax.axis_index("pcol")
    local_rows = top_inverse.shape[0]
    block_rows = local_rows // B
    own_parents = panel_one.shape[1] // B
    own_children = 2 * own_parents
    slab_rows = B // row_count
    rows_one = panel_one.shape[0]
    rows_two = panel_two.shape[0]
    first_block = row_index * block_rows
    mine_one = lax.dynamic_slice_in_dim(sets_one, col_index * own_parents, own_parents, 0)
    mine_two = lax.dynamic_slice_in_dim(sets_two, col_index * own_children, own_children, 0)
    inverse_rows = lax.all_gather(top_inverse, "pcol", axis=1, tiled=True)
    chosen_one = jnp.take(inverse_rows, column_index(mine_one), axis=1)
    chosen_two = jnp.take(inverse_rows, column_index(mine_two), axis=1)
    empty_one = jnp.zeros((local_rows, own_parents, B), jnp.float32)
    empty_two = jnp.zeros((local_rows, own_children, B), jnp.float32)
    prod_one = fold_rows(
        empty_one, lax.all_gather(panel_one, "prow", axis=0, tiled=True), chosen_one
    )
    prod_two = fold_rows(
        empty_two, lax.all_gather(panel_two, "prow", axis=0, tiled=True), chosen_two
    )
    place_one = placement(mine_one, first_block, block_rows)
    place_two = placement(mine_two, first_block, block_rows)
    prod_one_b = prod_one.reshape(block_rows, B, own_parents, B)
    prod_two_b = prod_two.reshape(block_rows, B, own_children, B)
    father_prod = jnp.broadcast_to(
        prod_one_b[:, :, :, None, :], (block_rows, B, own_parents, 2, B)
    ).reshape(block_rows, B, own_children, B)
    span_one = mine_one.shape[1]
    span_two = mine_two.shape[1]
    term_one = -jnp.einsum("jsq,qbje->sbje", place_one, prod_one_b, precision=EXACT).reshape(
        span_one * B, own_parents * B
    )
    term_two = jnp.einsum("csq,qbce->sbce", place_two, prod_two_b, precision=EXACT).reshape(
        span_two * B, own_children * B
    )
    term_upper = -jnp.einsum("csq,qbce->sbce", place_two, father_prod, precision=EXACT).reshape(
        span_two * B, own_children * B
    )
    below_one, reach_two, upper = (
        lax.psum_scatter(term_one, "prow", scatter_dimension=0, tiled=True),
        lax.psum_scatter(term_two, "prow", scatter_dimension=0, tiled=True),
        lax.psum_scatter(term_upper, "prow", scatter_dimension=0, tiled=True),
    )
    parent_full = lax.all_gather(parent_rows, "prow", axis=0, tiled=True)
    parent = parent_full.reshape(B, own_children, B)
    parent_mine = parent_rows.reshape(slab_rows, own_children, B)
    upper_r = upper.reshape(rows_two, own_children, B)
    couple = jnp.einsum("kcb,bce->kce", upper_r, parent, precision=EXACT)
    below_two_r = -(reach_two.reshape(rows_two, own_children, B) + couple)
    below_two = below_two_r.reshape(rows_two, own_children * B)
    low_one_r = panel_one.reshape(rows_one, own_parents, B)
    below_one_r = below_one.reshape(rows_one, own_parents, B)
    low_two_r = panel_two.reshape(rows_two, own_children, B)
    square_one = jnp.einsum("kjb,kje->bje", low_one_r, below_one_r, precision=EXACT).reshape(
        B, own_parents * B
    )
    cross = jnp.einsum("kcb,kce->bce", upper_r, low_two_r, precision=EXACT)
    second = jnp.einsum("kca,kce->ace", low_two_r, below_two_r, precision=EXACT)
    square_sum, cross_sum = (
        lax.psum_scatter(square_one, "prow", scatter_dimension=0, tiled=True),
        lax.psum_scatter(
            cross.reshape(B, own_children * B), "prow", scatter_dimension=0, tiled=True
        ),
    )
    corner_one = pivot_one - square_sum
    corner_c = twice_each(corner_one, slab_rows, own_parents)
    beside = -(
        jnp.einsum("acb,bce->ace", corner_c, parent, precision=EXACT)
        + cross_sum.reshape(slab_rows, own_children, B)
    )
    partial_value = jnp.einsum("bca,bce->ace", parent_mine, beside, precision=EXACT) + second
    partial_sum = lax.psum_scatter(
        partial_value.reshape(B, own_children * B), "prow", scatter_dimension=0, tiled=True
    )
    corner_two = pivot_two - partial_sum
    return (
        below_one,
        corner_one,
        below_two,
        beside.reshape(slab_rows, own_children * B),
        corner_two,
    )


def solution(mesh):
    in_specs = (
        P("prow", "pcol"),
        P("prow", "pcol"),
        P("prow", "pcol"),
        P("prow", "pcol"),
        P("prow", "pcol"),
        P("prow", "pcol"),
        P(),
        P(),
    )
    out_specs = (
        P("prow", "pcol"),
        P("prow", "pcol"),
        P("prow", "pcol"),
        P("prow", "pcol"),
        P("prow", "pcol"),
    )
    return jax.shard_map(
        on_device, mesh=mesh, in_specs=in_specs, out_specs=out_specs, check_vma=False
    )
```

profile of v0, /device:TPU:1, one launch (start us, length us, event | category | flops | bytes accessed | tf_op | source)
XLA Modules:
  0.0 780.4 jit_solution(955642143247539174)
XLA Ops:
  7.2 0.0 all-gather.4.cloned.1.call-start
  7.2 2.6 copy.56
  9.8 0.0 all-gather.4.cloned.1.call-update
  9.8 0.0 all-gather.6.cloned.1.call-start
  9.9 0.7 all-gather.6.cloned.1.call-update
  10.6 0.0 all-gather.8.cloned.1.call-start
  10.6 0.7 all-gather.8.cloned.1.call-update
  11.3 0.0 reduce-scatter.9.cloned.1.call-start
  11.4 0.7 broadcast_multiply_fusion.1
  12.1 0.1 broadcast_reduce_fusion
  12.3 0.1 add.197
  12.4 96.0 %all-gather.4.cloned.1.call-done = f32[512,8192]{0,1:T(8,128)} async-done(((f32[512,512]{0,1:T(8,128)}), f32[512,8192]{0,1:T(8,128)}) %all-gather.4.cloned.1.call-update) | async-done | bytes 16777232 | tf_op jit(solution)/shard_map/all_gather | solution.py:51
  108.4 14.5 %gather_fusion = f32[2560,512]{1,0:T(8,128)} fusion(f32[512,8192]{0,1:T(8,128)} %all-gather.4.cloned.1.call-done, s32[3072]{0:T(1024)S(1)} %pad_clamp_fusion.1), kind=kCustom, calls=%fused_computation | custom fusion | bytes 10496000 | tf_op jit(solution)/shard_map/jit(_take)/gather | solution.py:52
  122.9 51.3 %all-gather.6.cloned.1.call-done = f32[2560,256]{1,0:T(8,128)} async-done(((f32[160,256]{1,0:T(8,128)}), f32[2560,256]{1,0:T(8,128)}) %all-gather.6.cloned.1.call-update) | async-done | bytes 2621456 | tf_op jit(solution)/shard_map/all_gather | solution.py:57
  174.3 12.0 %fusion.3 = f32[512,256]{1,0:T(8,128)S(1)} fusion(f32[2560,256]{1,0:T(8,128)} %all-gather.6.cloned.1.call-done, f32[2560,512]{1,0:T(8,128)} %gather_fusion, pred[2560]{0:T(1024)(128)(4,1)S(1)} %compare_and_fusion.1), kind=kOutput, calls=%fused_computation.5 | convolution fusion | flops 4027842560 | bytes 8391168 | tf_op jit(solution)/shard_map/rjk,kje->rje/dot_general | solution.py:32
  186.2 2.1 negate_bitcast_fusion.1
  188.3 3.1 copy.58
  191.4 0.0 reduce-scatter.9.cloned.1.call-update
  191.4 0.2 reduce-scatter.13.cloned.1.call-start
  191.7 0.1 broadcast_multiply_fusion
  191.7 0.1 copy.64
  191.8 0.4 copy.57
  192.3 2.2 negate_bitcast_fusion
  194.4 2.0 copy.68
  196.5 1.7 copy.100
  198.2 0.0 reduce-scatter.13.cloned.1.call-update
  198.2 0.0 reduce-scatter.11.cloned.1.call-start
  198.2 0.1 copy.60
  198.3 0.1 add.213
  198.5 0.1 broadcast_bitcast_fusion
  198.6 39.3 %all-gather.8.cloned.1.call-done = f32[1280,512]{1,0:T(8,128)} async-done(((f32[80,512]{1,0:T(8,128)}), f32[1280,512]{1,0:T(8,128)}) %all-gather.8.cloned.1.call-update) | async-done | bytes 2621456 | tf_op jit(solution)/shard_map/all_gather | solution.py:60
  237.9 2.1 copy.62
  240.1 14.5 %gather_fusion.1 = f32[2560,512]{1,0:T(8,128)} fusion(f32[512,8192]{0,1:T(8,128)} %all-gather.4.cloned.1.call-done, s32[3072]{0:T(1024)S(1)} %pad_clamp_fusion), kind=kCustom, calls=%fused_computation.1 | custom fusion | bytes 10496000 | tf_op jit(solution)/shard_map/jit(_take)/gather | solution.py:53
  254.5 5.9 copy.61
  260.4 6.3 fusion
  266.8 2.7 convolution_bitcast_fusion
  269.4 2.0 copy.66
  271.5 1.7 copy.99
  273.3 0.0 reduce-scatter.19.cloned.1.call-start
  273.3 55.9 %reduce-scatter.9.cloned.1.call-done = f32[160,256]{1,0:T(8,128)} async-done(((f32[2560,256]{1,0:T(8,128)}), f32[160,256]{1,0:T(8,128)}) %reduce-scatter.9.cloned.1.call-update) | async-done | bytes 163856 | tf_op jit(solution)/shard_map/reduce_scatter | solution.py:81
  329.2 1.6 convolution_bitcast_fusion.1
  330.8 0.8 copy.89
  331.6 0.0 reduce-scatter.15.cloned.1.call-start
  331.7 88.9 %reduce-scatter.13.cloned.1.call-done = f32[80,512]{1,0:T(8,128)} async-done(((f32[1280,512]{1,0:T(8,128)}), f32[80,512]{1,0:T(8,128)}) %reduce-scatter.13.cloned.1.call-update) | async-done | bytes 163856 | tf_op jit(solution)/shard_map/reduce_scatter | solution.py:83
  420.6 1.6 fusion.17
  422.2 1.0 copy.78
  423.3 0.0 reduce-scatter.17.cloned.1.call-start
  423.3 0.1 copy.59
  423.4 41.8 %all_gather.15 = f32[256,512]{1,0:T(8,128)S(1)} all-gather(f32[16,512]{1,0:T(8,128)S(1)} %copy-done.3), channel_id=1, replica_groups=mesh['prow'=16,'pcol'=16] {'prow'}, dimensions={0}, use_global_device_ids=true | all-gather | bytes 557056 | tf_op jit(solution)/shard_map/all_gather | solution.py:85
  465.2 0.2 copy.69
  465.5 47.4 %reduce-scatter.11.cloned.1.call-done = f32[80,512]{1,0:T(8,128)} async-done(((f32[1280,512]{1,0:T(8,128)}), f32[80,512]{1,0:T(8,128)}) %reduce-scatter.11.cloned.1.call-update) | async-done | bytes 163856 | tf_op jit(solution)/shard_map/reduce_scatter | solution.py:82
  512.9 1.5 fusion.10
  514.4 0.6 fusion.15
  515.0 83.3 %reduce-scatter.19.cloned.1.call-done = f32[16,256]{1,0:T(8,128)} async-done(((f32[256,256]{1,0:T(8,128)}), f32[16,256]{1,0:T(8,128)}) %reduce-scatter.19.cloned.1.call-update) | async-done | bytes 16400
  598.4 0.8 copy.90
  599.2 0.1 copy.84
  599.3 86.3 %reduce-scatter.15.cloned.1.call-done = f32[16,512]{1,0:T(8,128)} async-done(((f32[256,512]{1,0:T(8,128)}), f32[16,512]{1,0:T(8,128)}) %reduce-scatter.15.cloned.1.call-update) | async-done | bytes 32784 | tf_op jit(solution)/shard_map/reduce_scatter | solution.py:102
  685.6 1.3 fusion.12
  686.9 0.6 convolution_add_fusion
  687.5 1.0 copy.83
  688.6 0.7 copy.96
  689.2 0.6 copy.97
  689.8 82.6 %reduce-scatter.17.cloned.1.call-done = f32[16,512]{1,0:T(8,128)} async-done(((f32[256,512]{1,0:T(8,128)}), f32[16,512]{1,0:T(8,128)}) %reduce-scatter.17.cloned.1.call-update) | async-done | bytes 32784 | tf_op jit(solution)/shard_map/reduce_scatter | solution.py:113
  772.5 1.4 sub.7
  (38 shorter events, 0.3 us)
Async XLA Ops:
  7.2 101.3 %all-gather.4.cloned.1.call-start = ((), (), s32[]{:S(2)}) async-start(), calls=%async_computation.6 | async-start | bytes 17825792 | tf_op jit(solution)/shard_map/all_gather | solution.py:51
  9.8 164.4 %all-gather.6.cloned.1.call-start = ((), (), s32[]{:S(2)}) async-start(), calls=%async_computation.7 | async-start | bytes 2785280 | tf_op jit(solution)/shard_map/all_gather | solution.py:57
  10.6 227.3 %all-gather.8.cloned.1.call-start = ((), (), s32[]{:S(2)}) async-start(), calls=%async_computation.9 | async-start | bytes 2785280 | tf_op jit(solution)/shard_map/all_gather | solution.py:60
  11.3 317.8 %reduce-scatter.9.cloned.1.call-start = ((), (), s32[]{:S(2)}) async-start(), calls=%async_computation.8 | async-start | bytes 2785280 | tf_op jit(solution)/shard_map/reduce_scatter | solution.py:81
  188.3 3.3 copy-start.7
  191.4 229.2 %reduce-scatter.13.cloned.1.call-start = ((), (), s32[]{:S(2)}) async-start(), calls=%async_computation.11 | async-start | bytes 2785280 | tf_op jit(solution)/shard_map/reduce_scatter | solution.py:83
  198.2 314.7 %reduce-scatter.11.cloned.1.call-start = ((), (), s32[]{:S(2)}) async-start(), calls=%async_computation.10 | async-start | bytes 2785280 | tf_op jit(solution)/shard_map/reduce_scatter | solution.py:82
  271.5 57.7 %copy-start.1 = (f32[160,256]{1,0:T(8,128)S(1)}, f32[160,256]{1,0:T(8,128)}, u32[]{:S(2)}) copy-start(f32[160,256]{1,0:T(8,128)} %param.9) | copy-start | bytes 491524
  271.5 149.1 %copy-start = (f32[80,512]{1,0:T(8,128)S(1)}, f32[80,512]{1,0:T(8,128)}, u32[]{:S(2)}) copy-start(f32[80,512]{1,0:T(8,128)} %param.10) | copy-start | bytes 491524
  273.2 150.1 %copy-start.6 = (f32[16,256]{1,0:T(8,128)S(1)}, f32[16,256]{1,0:T(8,128)}, u32[]{:S(2)}) copy-start(f32[16,256]{1,0:T(8,128)} %param.12) | copy-start | bytes 49156
  273.2 150.2 %copy-start.3 = (f32[16,512]{1,0:T(8,128)S(1)}, f32[16,512]{1,0:T(8,128)}, u32[]{:S(2)}) copy-start(f32[16,512]{1,0:T(8,128)} %param.11) | copy-start | bytes 98308
  273.3 325.1 %reduce-scatter.19.cloned.1.call-start = ((), (), s32[]{:S(2)}) async-start(), calls=%async_computation.14 | async-start | bytes 278528
  331.6 354.0 %reduce-scatter.15.cloned.1.call-start = ((), (), s32[]{:S(2)}) async-start(), calls=%async_computation.12 | async-start | bytes 557056 | tf_op jit(solution)/shard_map/reduce_scatter | solution.py:102
  420.6 92.3 %copy-start.2 = (f32[80,512]{1,0:T(8,128)S(1)}, f32[80,512]{1,0:T(8,128)}, u32[]{:S(2)}) copy-start(f32[80,512]{1,0:T(8,128)} %reduce-scatter.13.cloned.1.call-done) | copy-start | bytes 491524
  423.2 349.2 %copy-start.5 = (f32[16,512]{1,0:T(8,128)S(1)}, f32[16,512]{1,0:T(8,128)}, u32[]{:S(2)}) copy-start(f32[16,512]{1,0:T(8,128)} %param.13) | copy-start | bytes 98308
  423.3 349.2 %reduce-scatter.17.cloned.1.call-start = ((), (), s32[]{:S(2)}) async-start(), calls=%async_computation.13 | async-start | bytes 557056 | tf_op jit(solution)/shard_map/reduce_scatter | solution.py:113
  599.3 174.6 %copy-start.4 = (f32[16,256]{1,0:T(8,128)}, f32[16,256]{1,0:T(8,128)S(1)}, u32[]{:S(2)}) copy-start(f32[16,256]{1,0:T(8,128)S(1)} %copy.84) | copy-start | bytes 49156
Sparse Core Ops, SparseCore 0:
  10.0 98.4 all-gather.3
  110.9 63.3 all-gather.5
  176.7 61.1 all-gather.7
  241.9 87.1 reduce-scatter.8
  332.6 87.9 reduce-scatter.12
  424.1 88.7 reduce-scatter.10
  516.4 81.9 reduce-scatter.18
  602.3 83.3 reduce-scatter.14
  689.1 83.3 reduce-scatter.16
where the time goes:
time: 782 us; the launch traced here: 780 us
  waiting for transfers between devices  633 us (81%)
  local copies, waits for them, and re-layouts  56.5 us (7%)
  blocking collectives  41.8 us (5%)
  matrix products  32.4 us (4%)
  between operations  14.2 us (2%)
    all_gather x1, waiting for transfers between devices, on_device(): inverse_rows = lax.all_gather(top_inverse, 'pcol', axis=1, tiled=True)  96 us
    reduce_scatter x1, waiting for transfers between devices, on_device(): lax.psum_scatter(term_upper, 'prow', scatter_dimension=0, tiled=True)  88.9 us
    reduce_scatter x1, waiting for transfers between devices, on_device(): lax.psum_scatter(cross.reshape(B, own_children * B), 'prow', scatter_dime...  86.3 us
    unnamed x10, waiting for transfers between devices  84.8 us
    reduce_scatter x1, waiting for transfers between devices, on_device(): lax.psum_scatter(partial_value.reshape(B, own_children * B), 'prow', scat...  82.6 us
    reduce_scatter x1, waiting for transfers between devices, on_device(): lax.psum_scatter(term_one, 'prow', scatter_dimension=0, tiled=True)  55.9 us
    all_gather x1, waiting for transfers between devices, on_device(): lax.all_gather(panel_one, 'prow', axis=0, tiled=True)  51.3 us
    reduce_scatter x1, waiting for transfers between devices, on_device(): lax.psum_scatter(term_two, 'prow', scatter_dimension=0, tiled=True)  47.4 us
  transfers between devices with their start and end apart: 9, of which 9 were waited for; matrix products, arithmetic and copies ran while one was open for 11% of the time, Pallas kernels for 0%

commit v1 on v0

v1 whole, which is shorter than its diff:
```python
import functools

import jax
import jax.numpy as jnp
from jax import lax
from jax.experimental import pallas as pl
from jax.experimental.pallas import tpu as pltpu
from jax.sharding import PartitionSpec as P

MESH = pl.DeviceIdType.MESH
EXACT = lax.Precision.HIGHEST
F32 = jnp.float32


def mm(a, b):
    return jnp.dot(a, b, precision=EXACT, preferred_element_type=F32)


def mm_t(a, b):
    return lax.dot_general(
        a, b, (((0,), (0,)), ((), ())), precision=EXACT, preferred_element_type=F32
    )


def kernel(
    cfg,
    sets_one, sets_two, top, panel_one, panel_two, parent, pivot_one, pivot_two,
    below_one, corner_one, below_two, beside, corner_two,
    arows, zs, packed, landed, grid, l1, l2, pf,
    acc1, acc2, low1, low2, dir2, upper, b2s, part, sums, out1, out2,
    a_send, a_recv, b_send, b_recv, c_send, c_recv,
    g_send, g_recv, h_send, h_recv, own_sem, s_send, s_recv, o1_send, o1_recv, o2_send, o2_recv,
):
    nr, nc, ny, B, S1, S2 = cfg
    nz = nr // ny
    sub = B // nr
    H = max(B // 128, 1)
    LN = B // H
    r = lax.axis_index("prow")
    c = lax.axis_index("pcol")
    zi = r // ny
    yi = r % ny
    nbr = top.shape[0]
    npc = S1 * S1 * H
    rows1 = S1 * sub
    rows2 = S2 * sub

    def to_row(d):
        return (d, c)

    def to_col(d):
        return (r, d)

    def each(n, f):
        def body(k, _):
            f(k)
            return 0
        lax.fori_loop(0, n, body, 0)

    def rcopy(src, dst, ss, rs, dev):
        return pltpu.make_async_remote_copy(
            src_ref=src, dst_ref=dst, send_sem=ss, recv_sem=rs, device_id=dev, device_id_type=MESH
        )

    barrier = pltpu.get_barrier_semaphore()

    def greet_rows(k):
        pl.semaphore_signal(barrier, inc=1, device_id=to_row((r + k + 1) % nr), device_id_type=MESH)

    def greet_cols(k):
        pl.semaphore_signal(barrier, inc=1, device_id=to_col((c + k + 1) % nc), device_id_type=MESH)

    each(nr - 1, greet_rows)
    each(nc - 1, greet_cols)
    pl.semaphore_wait(barrier, nr + nc - 2)

    own = [
        pltpu.make_async_copy(panel_one, l1.at[pl.ds(r * rows1, rows1)], own_sem.at[0]),
        pltpu.make_async_copy(panel_two, l2.at[pl.ds(r * rows2, rows2)], own_sem.at[1]),
        pltpu.make_async_copy(parent, pf.at[pl.ds(r * sub, sub)], own_sem.at[2]),
    ]
    for cp in own:
        cp.start()

    def z_copies(dz):
        dev = to_row(((zi + dz) % nz) * ny + yi)
        i = dz - 1
        return [
            rcopy(panel_one, l1.at[pl.ds(r * rows1, rows1)], g_send.at[i, 0], g_recv.at[i, 0], dev),
            rcopy(panel_two, l2.at[pl.ds(r * rows2, rows2)], g_send.at[i, 1], g_recv.at[i, 1], dev),
            rcopy(parent, pf.at[pl.ds(r * sub, sub)], g_send.at[i, 2], g_recv.at[i, 2], dev),
        ]

    for dz in range(1, nz):
        for cp in z_copies(dz):
            cp.start()

    def a_copy(k):
        d = (r + k + 1) % nr
        return rcopy(top.at[:, d], arows.at[pl.ds(r * nbr, nbr)], a_send.at[k], a_recv.at[k], to_row(d))

    each(nr - 1, lambda k: a_copy(k).start())
    own_a = pltpu.make_async_copy(top.at[:, r], arows.at[pl.ds(r * nbr, nbr)], own_sem.at[3])
    own_a.start()

    for cp in own:
        cp.wait()

    def y_copies(dz, dy):
        s = ((zi - dz + nz) % nz) * ny + yi
        dev = to_row(zi * ny + (yi + dy) % ny)
        i = dz * (ny - 1) + dy - 1
        a = l1.at[pl.ds(s * rows1, rows1)]
        b = l2.at[pl.ds(s * rows2, rows2)]
        p = pf.at[pl.ds(s * sub, sub)]
        return [
            rcopy(a, a, h_send.at[i, 0], h_recv.at[i, 0], dev),
            rcopy(b, b, h_send.at[i, 1], h_recv.at[i, 1], dev),
            rcopy(p, p, h_send.at[i, 2], h_recv.at[i, 2], dev),
        ]

    for dz in range(nz):
        if dz > 0:
            for cp in z_copies(dz):
                cp.wait_recv()
        for dy in range(1, ny):
            for cp in y_copies(dz, dy):
                cp.start()

    own_a.wait()
    each(nr - 1, lambda k: a_copy(k).wait_recv())

    def b_copy(k):
        d = (c + k + 1) % nc
        return rcopy(arows.at[:, d], zs.at[c], b_send.at[k], b_recv.at[k], to_col(d))

    each(nc - 1, lambda k: b_copy(k).start())
    own_b = pltpu.make_async_copy(arows.at[:, c], zs.at[c], own_sem.at[4])
    own_b.start()
    own_b.wait()
    each(nc - 1, lambda k: b_copy(k).wait_recv())

    nbc = arows.shape[2]

    def pack(j):
        places = [sets_one[j, s] for s in range(S1)]
        cols = [(lax.div(q, nbc), lax.rem(q, nbc)) for q in places]
        for a in range(S1):
            for b in range(S1):
                i = (a * S1 + b) * H
                packed[j, i : i + H, :] = zs[cols[b][0], places[a], cols[b][1]]

    def c_copy(k):
        d = (c + k + 1) % nc
        return rcopy(packed.at[d], landed.at[pl.ds(c * npc, npc)], c_send.at[k], c_recv.at[k], to_col(d))

    def pack_send(k):
        pack((c + k + 1) % nc)
        c_copy(k).start()

    each(nc - 1, pack_send)
    pack(c)
    own_c = pltpu.make_async_copy(packed.at[c], landed.at[pl.ds(c * npc, npc)], own_sem.at[5])
    own_c.start()
    own_c.wait()
    each(nc - 1, lambda k: c_copy(k).wait_recv())

    def assemble(b):
        for a in range(S1):
            for h in range(H):
                i = (a * S1 + b) * H + h
                grid[b, a * sub : (a + 1) * sub, h * LN : (h + 1) * LN] = landed[pl.ds(i, nc, stride=npc), :]

    each(S1, assemble)

    for dz in range(nz):
        for dy in range(1, ny):
            for cp in y_copies(dz, dy):
                cp.wait_recv()

    acc1[...] = jnp.zeros_like(acc1)

    def step_one(b):
        acc1[...] -= mm(grid[b], l1[pl.ds(pl.multiple_of(b * B, B), B), :]).reshape(acc1.shape)

    each(S1, step_one)

    def o1_copy(a):
        g = a * nr + r
        return g // S1, rcopy(
            acc1.at[a], out1.at[pl.ds((g % S1) * sub, sub)],
            o1_send.at[a], o1_recv.at[g % S1], to_row(g // S1),
        )

    def o2_copy(t):
        g = t * nr + r
        return g // S2, rcopy(
            b2s.at[t], out2.at[pl.ds((g % S2) * sub, sub)],
            o2_send.at[t], o2_recv.at[g % S2], to_row(g // S2),
        )

    def send_out(n, copy, src, dst):
        def go(a):
            d, cp = copy(a)

            @pl.when(d != r)
            def _():
                cp.start()

            @pl.when(d == r)
            def _():
                at = ((a * nr + r) % n) * sub
                dst[pl.ds(pl.multiple_of(at, sub), sub), :] = src[a]

        each(n, go)

    def done_out(n, copy, src, dst, send, recv):
        def go(a):
            d, cp = copy(a)

            @pl.when(d != r)
            def _():
                cp.wait_send()

            s = (r * n + a) % nr

            @pl.when(s != r)
            def _():
                rcopy(src.at[0], dst.at[pl.ds(a * sub, sub)], send.at[a], recv.at[a], to_row(s)).wait_recv()

        each(n, go)

    send_out(S1, o1_copy, acc1, out1)

    for a in range(S1):
        low1[a * sub : (a + 1) * sub, :] = l1[pl.ds(pl.multiple_of(a * B + r * sub, sub), sub), :]
    for t in range(S2):
        low2[t * sub : (t + 1) * sub, :] = l2[pl.ds(pl.multiple_of(t * B + r * sub, sub), sub), :]

    square = mm_t(low1[...], acc1[...].reshape(S1 * sub, B))
    part[:, :, 0:B] = square.reshape(nr, sub, B)

    for ch in range(2):
        cs = slice(ch * B, (ch + 1) * B)
        pos = []
        for t in range(S2):
            want = sets_two[2 * c + ch, t]
            at = 0
            for s in range(S1):
                at = at + s * (1 - lax.min(lax.abs(sets_one[c, s] - want), 1))
            pos.append(lax.min(at, S1 - 1))
        acc2[...] = jnp.zeros_like(acc2)
        for t in range(S2):
            acc2[...] += mm(grid[pos[t]], l2[t * B : (t + 1) * B, cs]).reshape(acc2.shape)
        for t in range(S2):
            dir2[t * sub : (t + 1) * sub, :] = acc2[pos[t]]
            upper[t * sub : (t + 1) * sub, :] = acc1[pos[t]]
        pc = pf[:, cs]
        u = upper[...]
        l2c = low2[:, cs]
        b2 = -(dir2[...] + mm(u, pc))
        b2s[:, :, cs] = b2.reshape(S2, sub, B)
        cross = mm_t(u, l2c)
        part[:, :, B + ch * B : 2 * B + ch * B] = cross.reshape(nr, sub, B)
        inner = cross - mm(part[:, :, 0:B].reshape(B, B), pc)
        last = mm_t(pc, inner) - mm_t(l2c, b2) + mm_t(parent[:, cs], mm(pivot_one[...], pc))
        part[:, :, 3 * B + ch * B : 4 * B + ch * B] = last.reshape(nr, sub, B)

    def s_copy(k):
        d = (r + k + 1) % nr
        return rcopy(part.at[d], sums.at[r], s_send.at[k], s_recv.at[k], to_row(d))

    each(nr - 1, lambda k: s_copy(k).start())
    sums[r] = part[r]
    send_out(S2, o2_copy, b2s, out2)
    each(nr - 1, lambda k: s_copy(k).wait_recv())

    total = sums[0]
    for k in range(1, nr):
        total = total + sums[k]
    corner = pivot_one[...] - total[:, 0:B]
    corner_one[...] = corner
    for ch in range(2):
        cs = slice(ch * B, (ch + 1) * B)
        beside[:, cs] = -(mm(corner, pf[:, cs]) + total[:, B + ch * B : 2 * B + ch * B])
        corner_two[:, cs] = pivot_two[:, cs] + total[:, 3 * B + ch * B : 4 * B + ch * B]

    done_out(S1, o1_copy, acc1, out1, o1_send, o1_recv)
    done_out(S2, o2_copy, b2s, out2, o2_send, o2_recv)
    below_one[...] = out1[...]
    below_two[...] = out2[...]

    each(nr - 1, lambda k: a_copy(k).wait_send())
    each(nc - 1, lambda k: b_copy(k).wait_send())
    each(nc - 1, lambda k: c_copy(k).wait_send())
    each(nr - 1, lambda k: s_copy(k).wait_send())
    for dz in range(1, nz):
        for cp in z_copies(dz):
            cp.wait_send()
    for dz in range(nz):
        for dy in range(1, ny):
            for cp in y_copies(dz, dy):
                cp.wait_send()


def on_device(ny, top, panel_one, panel_two, parent, pivot_one, pivot_two, sets_one, sets_two):
    nr = lax.axis_size("prow")
    nc = lax.axis_size("pcol")
    S1 = sets_one.shape[1]
    S2 = sets_two.shape[1]
    B = panel_one.shape[1]
    sub = B // nr
    H = max(B // 128, 1)
    LN = B // H
    NB = top.shape[0] * nr // B
    nbr, nbc = NB // nr, NB // nc
    npc = S1 * S1 * H
    nz = nr // ny
    cfg = (nr, nc, ny, B, S1, S2)
    top = top.reshape(nbr, nr, sub, nbc, H, LN)
    vmem = pl.BlockSpec(memory_space=pltpu.VMEM)
    smem = pl.BlockSpec(memory_space=pltpu.SMEM)
    V = lambda *s: pltpu.VMEM(s, F32)
    D = lambda *s: pltpu.SemaphoreType.DMA(s)
    out = lambda *s: jax.ShapeDtypeStruct(s, F32)
    return pl.pallas_call(
        functools.partial(kernel, cfg),
        out_shape=(
            out(S1 * sub, B), out(sub, B), out(S2 * sub, 2 * B), out(sub, 2 * B), out(sub, 2 * B),
        ),
        in_specs=[smem, smem] + [vmem] * 6,
        out_specs=(vmem,) * 5,
        scratch_shapes=[
            V(NB, sub, nbc, H, LN),
            V(nc, NB, nbc, H, LN),
            V(nc, npc, LN),
            V(nc * npc, LN),
            V(S1, S1 * sub, B),
            V(S1 * B, B),
            V(S2 * B, 2 * B),
            V(B, 2 * B),
            V(S1, sub, B),
            V(S1, sub, B),
            V(S1 * sub, B),
            V(S2 * sub, 2 * B),
            V(S2 * sub, B),
            V(S2 * sub, B),
            V(S2, sub, 2 * B),
            V(nr, sub, 5 * B),
            V(nr, sub, 5 * B),
            V(S1 * sub, B),
            V(S2 * sub, 2 * B),
            D(nr - 1), D(nr - 1), D(nc - 1), D(nc - 1), D(nc - 1), D(nc - 1),
            D(nz - 1, 3), D(nz - 1, 3), D(nz * (ny - 1), 3), D(nz * (ny - 1), 3), D(6),
            D(nr - 1), D(nr - 1), D(S1), D(S1), D(S2), D(S2),
        ],
        compiler_params=pltpu.CompilerParams(
            collective_id=0, has_side_effects=True, vmem_limit_bytes=56 * 1024 * 1024
        ),
    )(sets_one, sets_two, top, panel_one, panel_two, parent, pivot_one, pivot_two)


def solution(mesh):
    spec = P("prow", "pcol")
    return jax.shard_map(
        functools.partial(on_device, 4),
        mesh=mesh,
        in_specs=(spec,) * 6 + (P(), P()),
        out_specs=(spec,) * 5,
        check_vma=False,
    )
```

time: 782 us -> 163 us (0.21)
  the two profiles are of different devices: /device:TPU:1 before, /device:TPU:15 now
where the time goes in v1:
time: 163 us; the launch traced here: 162 us
  Pallas kernels  153 us (94%)
  local copies, waits for them, and re-layouts  8.6 us (5%)
    pallas_call x1, Pallas kernels, on_device(): pl.pallas_call(functools.partial(kernel, cfg), out_shape=(out(S1 * sub, B...  153 us
    unnamed x14, local copies, waits for them, and re-layouts  5.76 us

profile of v1, /device:TPU:15, one launch (start us, length us, event | category | flops | bytes accessed | tf_op | source)
XLA Modules:
  0.0 162.3 jit_solution(10129331004271515749)
XLA Ops:
  0.6 1.4 copy.13.sets_two
  2.0 2.8 %reshape.13.top = f32[2,16,16,2,2,128]{5,4,3,2,1,0:T(2,128)} reshape(f32[512,512]{1,0:T(8,128)} %param.8) | data formatting | bytes 2097152 | tf_op jit(solution)/shard_map/reshape | solution.py:320
  4.8 153.0 %shard_map.119 = (f32[160,256]{1,0:T(8,128)}, f32[16,256]{1,0:T(8,128)}, f32[80,512]{1,0:T(8,128)}, f32[16,512]{1,0:T(8,128)}, f32[16,512]{1,0:T(8,128)}) custom-call(s32[16,10]{1,0:T(8,128)} %sets_one.1, s32[32,5]{1,0:T(8,128)} %copy.13.sets_two, f32[2,16,16,2,2,128]{5,4,3,2,1,0:T(2,128)} %reshape.13.top, f32[160,256]{1,0:T(8,128)} %panel_one.1, ...), custom_call_target="tpu_custom_call" | custom-call | tf_op jit(solution)/shard_map/pallas_call | solution.py:326
  157.8 0.0 copy-start.3
  157.9 0.0 copy-start
  157.9 1.6 %copy.19 = f32[160,256]{1,0:T(8,128)} copy(f32[160,256]{1,0:T(8,128)} %get-tuple-element.10) | data formatting | bytes 327680
  159.5 0.0 copy-done.3
  159.5 0.6 copy.20
  160.1 0.0 copy-done
  160.1 0.0 copy-start.2
  160.1 0.7 copy.21
  160.8 0.1 copy-done.2
  160.9 0.0 copy-start.1
  160.9 0.6 copy.22
  161.5 0.2 copy-done.1
  161.6 0.6 copy.23
Async XLA Ops:
  157.8 1.7 %copy-start.3 = (f32[16,256]{1,0:T(8,128)S(1)}, f32[16,256]{1,0:T(8,128)}, u32[]{:S(2)}) copy-start(f32[16,256]{1,0:T(8,128)} %get-tuple-element.11) | copy-start | bytes 49156
  157.9 2.3 %copy-start = (f32[80,512]{1,0:T(8,128)S(1)}, f32[80,512]{1,0:T(8,128)}, u32[]{:S(2)}) copy-start(f32[80,512]{1,0:T(8,128)} %get-tuple-element.12) | copy-start | bytes 491524
  160.1 0.8 copy-start.2
  160.9 0.8 copy-start.1

commit v2 on v1

v2 whole, which is shorter than its diff:
```python
import functools

import jax
import jax.numpy as jnp
from jax import lax
from jax.experimental import pallas as pl
from jax.experimental.pallas import tpu as pltpu
from jax.sharding import PartitionSpec as P

MESH = pl.DeviceIdType.MESH
EXACT = lax.Precision.HIGHEST
F32 = jnp.float32
DIMS = (4, 4, 4, 2, 2)


def mm(a, b):
    return jnp.dot(a, b, precision=EXACT, preferred_element_type=F32)


def mm_t(a, b):
    return lax.dot_general(
        a, b, (((0,), (0,)), ((), ())), precision=EXACT, preferred_element_type=F32
    )


def kernel(
    cfg,
    sets_one, sets_two, top, panel_one, panel_two, parent, pivot_one, pivot_two,
    below_one, corner_one, below_two, beside, corner_two,
    arows, zs, packed, landed, grid, bundle, lg, l1, l2, pf,
    acc1, acc2, low1, low2, dir2, upper, b2s, part, sibpart, comb, sums, out1, out2, fin, fin_in, out1_in, out2_in,
    swap_sem, a_send, a_recv, b_send, b_recv, c_send, c_recv,
    ring_send, ring_recv, sib_send, sib_recv, own_sem,
    x_send, x_recv, s_send, s_recv, o1_send, o1_recv, o2_send, o2_recv, back_send, back_recv,
):
    B, S1, S2 = cfg
    nx, ny, nzh, nzl, nk = DIMS
    nz = nzh * nzl
    nr = nz * nk
    nc = nx * ny
    sub = B // nr
    H = max(B // 128, 1)
    LN = B // H
    npc = S1 * S1 * H
    share1 = S1 * sub
    share2 = S2 * sub
    gathered = share1 + 2 * share2 + 2 * sub
    half = gathered // 2
    nq = top.shape[0]
    prow = lax.axis_index("prow")
    pcol = lax.axis_index("pcol")
    zh, y = prow // ny, prow % ny
    zl, x, core = pcol // (nx * nk), (pcol // nk) % nx, pcol % nk
    z = zh * nzl + zl
    me = z * nk + core
    line = x * ny + y

    def device(x, y, z, core):
        return ((z // nzl) * ny + y, (z % nzl) * (nx * nk) + x * nk + core)

    def to_member(m):
        return device(x, y, m // nk, m % nk)

    def to_line(d):
        return device(d // ny, d % ny, z, core)

    def node_of(d):
        dy = d % ny
        return (dy // nk) * (nx * nk) + (d // ny) * nk + dy % nk

    partner = device(x, zl * nk + core, zh * nzl + y // nk, y % nk)
    away = y != zl * nk + core
    sibling = device(x, y, z, 1 - core)

    def each(n, f):
        def body(k, _):
            f(k)
            return 0
        lax.fori_loop(0, n, body, 0)

    def rcopy(src, dst, ss, rs, dev):
        return pltpu.make_async_remote_copy(
            src_ref=src, dst_ref=dst, send_sem=ss, recv_sem=rs, device_id=dev, device_id_type=MESH
        )

    barrier = pltpu.get_barrier_semaphore()

    def greet(dev):
        pl.semaphore_signal(barrier, inc=1, device_id=dev, device_id_type=MESH)

    each(nr - 1, lambda k: greet(to_member((me + k + 1) % nr)))
    each(nc - 1, lambda k: greet(to_line((line + k + 1) % nc)))

    @pl.when(away)
    def _():
        greet(partner)

    bundle[0:share1, :] = panel_one[...]
    at = share1
    for ch in range(2):
        bundle[at : at + share2, :] = panel_two[:, ch * B : (ch + 1) * B]
        at += share2
    for ch in range(2):
        bundle[at : at + sub, :] = parent[:, ch * B : (ch + 1) * B]
        at += sub
    bundle[at : at + sub, :] = pivot_one[...]
    at += sub
    for ch in range(2):
        bundle[at : at + sub, :] = pivot_two[:, ch * B : (ch + 1) * B]
        at += sub

    pl.semaphore_wait(barrier, nr + nc - 2 + lax.min(lax.abs(y - (zl * nk + core)), 1))

    swap = rcopy(bundle, lg.at[prow], swap_sem.at[0], swap_sem.at[1], partner)

    @pl.when(away)
    def _():
        swap.start()

    def a_copy(k):
        d = (me + k + 1) % nr
        return rcopy(top.at[:, d], arows.at[pl.ds(me * nq, nq)], a_send.at[k], a_recv.at[k], to_member(d))

    each(nr - 1, lambda k: a_copy(k).start())
    own_a = pltpu.make_async_copy(top.at[:, me], arows.at[pl.ds(me * nq, nq)], own_sem.at[0])
    own_a.start()

    @pl.when(away)
    def _():
        swap.wait_recv()

    @pl.when(jnp.logical_not(away))
    def _():
        lg[prow] = bundle[...]

    steps = nz // 2

    def ring_copy(way, s):
        to = (z + way + nz) % nz
        owner = ((z - way * s + nz) % nz) * nk + core
        w = 0 if way == 1 else 1
        if s < steps - 1:
            rows = pl.ds(0, gathered)
        else:
            rows = pl.ds(w * half, half)
        ref = lg.at[owner, rows]
        return rcopy(ref, ref, ring_send.at[w, s], ring_recv.at[w, s], device(x, y, to, core))

    def sib_copy(way, s):
        w = 0 if way == 1 else 1
        owner = ((z - way * s + nz) % nz) * nk + core
        if s < steps:
            rows = pl.ds(0, gathered)
        else:
            rows = pl.ds(w * half, half)
        ref = lg.at[owner, rows]
        i = 0 if s == 0 else 1 + w * steps + s - 1
        return rcopy(ref, ref, sib_send.at[i], sib_recv.at[i], sibling)

    WAYS = (1, -1)

    def pass_on(s):
        for way in WAYS:
            ring_copy(way, s - 1).wait_recv()
            if s < steps:
                ring_copy(way, s).start()
            sib_copy(way, s).start()

    for way in WAYS:
        ring_copy(way, 0).start()
    sib_copy(1, 0).start()

    own_a.wait()
    each(nr - 1, lambda k: a_copy(k).wait_recv())

    nb = nr * nq

    def b_copy(k):
        d = (line + k + 1) % nc
        return rcopy(arows.at[:, d], zs.at[pl.ds(line * nb, nb)], b_send.at[k], b_recv.at[k], to_line(d))

    each(nc - 1, lambda k: b_copy(k).start())
    own_b = pltpu.make_async_copy(arows.at[:, line], zs.at[pl.ds(line * nb, nb)], own_sem.at[1])
    own_b.start()

    pass_on(1)

    own_b.wait()
    each(nc - 1, lambda k: b_copy(k).wait_recv())

    nbr = 2
    nbc = nq // nbr

    def pack(d):
        j = node_of(d)
        rows, cols = [], []
        for s in range(S1):
            q = sets_one[j, s]
            r = lax.div(q, nbr)
            rows.append(lax.rem(r, ny) * nb + lax.div(r, ny) * (nzl * nk * nq) + lax.rem(q, nbr) * nbc)
            c = lax.div(q, nbc)
            cc = lax.div(c, nk)
            cols.append(
                lax.rem(cc, nx) * (ny * nb) + lax.div(cc, nx) * (nk * nq) + lax.rem(c, nk) * nq + lax.rem(q, nbc)
            )
        for a in range(S1):
            for b in range(S1):
                i = (a * S1 + b) * H
                packed[d, i : i + H, :] = zs[rows[a] + cols[b]]

    def c_copy(k):
        d = (line + k + 1) % nc
        return rcopy(packed.at[d], landed.at[pl.ds(line * npc, npc)], c_send.at[k], c_recv.at[k], to_line(d))

    def pack_send(k):
        pack((line + k + 1) % nc)
        c_copy(k).start()

    each(nc - 1, pack_send)
    pack(line)
    own_c = pltpu.make_async_copy(packed.at[line], landed.at[pl.ds(line * npc, npc)], own_sem.at[2])
    own_c.start()

    for s in range(2, steps + 1):
        pass_on(s)

    sib_copy(1, 0).wait_recv()
    for s in range(1, steps + 1):
        for way in WAYS:
            sib_copy(way, s).wait_recv()

    def spread(m):
        l1[pl.ds(m * share1, share1), :] = lg[m, 0:share1, :]
        for ch in range(2):
            o = share1 + ch * share2
            l2[ch, pl.ds(m * share2, share2), :] = lg[m, o : o + share2, :]
            o = share1 + 2 * share2 + ch * sub
            pf[ch, pl.ds(m * sub, sub), :] = lg[m, o : o + sub, :]

    each(nr, spread)

    own_c.wait()
    each(nc - 1, lambda k: c_copy(k).wait_recv())

    def assemble(b):
        for a in range(S1):
            for h in range(H):
                i = (a * S1 + b) * H + h
                grid[b, a * sub : (a + 1) * sub, h * LN : (h + 1) * LN] = landed[pl.ds(i, nc, stride=npc), :]

    each(S1, assemble)

    acc1[...] = jnp.zeros_like(acc1)

    def step_one(b):
        acc1[...] -= mm(grid[b], l1[pl.ds(pl.multiple_of(b * B, B), B), :]).reshape(acc1.shape)

    each(S1, step_one)

    def o1_copy(a):
        g = a * nr + me
        return g // S1, rcopy(
            acc1.at[a], out1.at[pl.ds((g % S1) * sub, sub)],
            o1_send.at[a], o1_recv.at[g % S1], to_member(g // S1),
        )

    def o2_copy(t):
        g = t * nr + me
        return g // S2, rcopy(
            b2s.at[t], out2.at[pl.ds((g % S2) * sub, sub)],
            o2_send.at[t], o2_recv.at[g % S2], to_member(g // S2),
        )

    def send_out(n, copy, src, dst):
        def go(a):
            d, cp = copy(a)

            @pl.when(d != me)
            def _():
                cp.start()

            @pl.when(d == me)
            def _():
                at = ((a * nr + me) % n) * sub
                dst[pl.ds(pl.multiple_of(at, sub), sub), :] = src[a]

        each(n, go)

    def take_out(n, src, dst, send, recv):
        def go(a):
            s = (me * n + a) % nr

            @pl.when(s != me)
            def _():
                rcopy(src.at[0], dst.at[pl.ds(a * sub, sub)], send.at[a], recv.at[a], to_member(s)).wait_recv()

        each(n, go)

    def done_out(n, copy):
        def go(a):
            d, cp = copy(a)

            @pl.when(d != me)
            def _():
                cp.wait_send()

        each(n, go)

    send_out(S1, o1_copy, acc1, out1)

    def x_copy(g, cs):
        return rcopy(part.at[:, 1 - core, :, cs], sibpart.at[:, :, cs], x_send.at[g], x_recv.at[g], sibling)

    def s_copy(g, cs, k):
        d = (z + k + 1) % nz
        return rcopy(comb.at[d, :, cs], sums.at[z, :, cs], s_send.at[g, k], s_recv.at[g, k], device(x, y, d, core))

    spans = [pl.ds(0, B), pl.ds(B, 2 * B), pl.ds(3 * B, 2 * B)]

    def combine(g):
        cs = spans[g]
        x_copy(g, cs).wait_recv()
        comb[:, :, cs] = part[:, core, :, cs] + sibpart[:, :, cs]
        for k in range(nz - 1):
            s_copy(g, cs, k).start()

    node = node_of(line)
    for a in range(S1):
        low1[a * sub : (a + 1) * sub, :] = l1[pl.ds(pl.multiple_of(a * B + me * sub, sub), sub), :]
    square = mm_t(low1[...], acc1[...].reshape(S1 * sub, B))
    part[:, :, :, 0:B] = square.reshape(nz, nk, sub, B)
    x_copy(0, spans[0]).start()
    pivot1 = lg[me, gathered : gathered + sub, :]

    for ch in range(2):
        for t in range(S2):
            low2[t * sub : (t + 1) * sub, :] = l2[ch, pl.ds(pl.multiple_of(t * B + me * sub, sub), sub), :]
        pos = []
        for t in range(S2):
            want = sets_two[2 * node + ch, t]
            at = 0
            for s in range(S1):
                at = at + s * (1 - lax.min(lax.abs(sets_one[node, s] - want), 1))
            pos.append(lax.min(at, S1 - 1))
        acc2[...] = jnp.zeros_like(acc2)
        for t in range(S2):
            acc2[...] += mm(grid[pos[t]], l2[ch, t * B : (t + 1) * B, :]).reshape(acc2.shape)
        for t in range(S2):
            dir2[t * sub : (t + 1) * sub, :] = acc2[pos[t]]
            upper[t * sub : (t + 1) * sub, :] = acc1[pos[t]]
        pc = pf[ch]
        u = upper[...]
        l2c = low2[...]
        b2 = -(dir2[...] + mm(u, pc))
        b2s[:, :, ch * B : (ch + 1) * B] = b2.reshape(S2, sub, B)
        cross = mm_t(u, l2c)
        inner = cross - mm(part[:, :, :, 0:B].reshape(B, B), pc)
        mine = pf[ch, pl.ds(pl.multiple_of(me * sub, sub), sub), :]
        last = mm_t(pc, inner) - mm_t(l2c, b2) + mm_t(mine, mm(pivot1, pc))
        o = B + 2 * ch * B
        part[:, :, :, o : o + B] = cross.reshape(nz, nk, sub, B)
        part[:, :, :, o + B : o + 2 * B] = last.reshape(nz, nk, sub, B)
        x_copy(ch + 1, spans[ch + 1]).start()
        combine(ch)

    send_out(S2, o2_copy, b2s, out2)
    combine(2)

    take_out(S1, acc1, out1, o1_send, o1_recv)
    take_out(S2, b2s, out2, o2_send, o2_recv)
    backs = [
        rcopy(out1, out1_in, back_send.at[0], back_recv.at[0], partner),
        rcopy(out2, out2_in, back_send.at[1], back_recv.at[1], partner),
        rcopy(fin, fin_in, back_send.at[2], back_recv.at[2], partner),
    ]

    @pl.when(away)
    def _():
        backs[0].start()
        backs[1].start()

    for g in range(3):
        for k in range(nz - 1):
            s_copy(g, spans[g], k).wait_recv()

    total = comb[z]
    for k in range(1, nz):
        total = total + sums[(z + k) % nz]
    corner = pivot1 - total[:, 0:B]
    fin[:, 0:B] = corner
    for ch in range(2):
        o = B + 2 * ch * B
        p2 = gathered + sub + ch * sub
        fin[:, (1 + ch) * B : (2 + ch) * B] = -(mm(corner, pf[ch]) + total[:, o : o + B])
        fin[:, (3 + ch) * B : (4 + ch) * B] = lg[me, p2 : p2 + sub, :] + total[:, o + B : o + 2 * B]

    def deliver(o1, o2, f):
        below_one[...] = o1[...]
        below_two[...] = o2[...]
        corner_one[...] = f[:, 0:B]
        beside[...] = f[:, B : 3 * B]
        corner_two[...] = f[:, 3 * B : 5 * B]

    @pl.when(away)
    def _():
        backs[2].start()
        for cp in backs:
            cp.wait_recv()
        deliver(out1_in, out2_in, fin_in)

    @pl.when(jnp.logical_not(away))
    def _():
        deliver(out1, out2, fin)

    @pl.when(away)
    def _():
        swap.wait_send()
        for cp in backs:
            cp.wait_send()

    each(nr - 1, lambda k: a_copy(k).wait_send())
    each(nc - 1, lambda k: b_copy(k).wait_send())
    each(nc - 1, lambda k: c_copy(k).wait_send())
    for way in WAYS:
        for s in range(steps):
            ring_copy(way, s).wait_send()
            sib_copy(way, s + 1).wait_send()
    sib_copy(1, 0).wait_send()
    for g in range(3):
        x_copy(g, spans[g]).wait_send()
        for k in range(nz - 1):
            s_copy(g, spans[g], k).wait_send()
    done_out(S1, o1_copy)
    done_out(S2, o2_copy)


def on_device(top, panel_one, panel_two, parent, pivot_one, pivot_two, sets_one, sets_two):
    nx, ny, nzh, nzl, nk = DIMS
    nz = nzh * nzl
    nr = nz * nk
    nc = nx * ny
    S1 = sets_one.shape[1]
    S2 = sets_two.shape[1]
    B = panel_one.shape[1]
    sub = B // nr
    H = max(B // 128, 1)
    LN = B // H
    nbr, nbc = top.shape[0] // B, top.shape[1] // B
    nq = nbr * nbc
    npc = S1 * S1 * H
    share1, share2 = S1 * sub, S2 * sub
    gathered = share1 + 2 * share2 + 2 * sub
    whole = gathered + 3 * sub
    steps = nz // 2
    cfg = (B, S1, S2)
    top = top.reshape(nbr, nr, sub, nbc, H, LN).transpose(0, 3, 1, 2, 4, 5).reshape(nq, nr, sub, H, LN)
    vmem = pl.BlockSpec(memory_space=pltpu.VMEM)
    smem = pl.BlockSpec(memory_space=pltpu.SMEM)
    V = lambda *s: pltpu.VMEM(s, F32)
    D = lambda *s: pltpu.SemaphoreType.DMA(s)
    out = lambda *s: jax.ShapeDtypeStruct(s, F32)
    return pl.pallas_call(
        functools.partial(kernel, cfg),
        out_shape=(
            out(share1, B), out(sub, B), out(share2, 2 * B), out(sub, 2 * B), out(sub, 2 * B),
        ),
        in_specs=[smem, smem] + [vmem] * 6,
        out_specs=(vmem,) * 5,
        scratch_shapes=[
            V(nr * nq, sub, H, LN),
            V(nc * nr * nq, H, LN),
            V(nc, npc, LN),
            V(nc * npc, LN),
            V(S1, share1, B),
            V(whole, B),
            V(nr, whole, B),
            V(S1 * B, B),
            V(2, S2 * B, B),
            V(2, B, B),
            V(S1, sub, B),
            V(S1, sub, B),
            V(share1, B),
            V(share2, B),
            V(share2, B),
            V(share2, B),
            V(S2, sub, 2 * B),
            V(nz, nk, sub, 5 * B),
            V(nz, sub, 5 * B),
            V(nz, sub, 5 * B),
            V(nz, sub, 5 * B),
            V(share1, B),
            V(share2, 2 * B),
            V(sub, 5 * B),
            V(sub, 5 * B),
            V(share1, B),
            V(share2, 2 * B),
            D(2),
            D(nr - 1), D(nr - 1), D(nc - 1), D(nc - 1), D(nc - 1), D(nc - 1),
            D(2, steps), D(2, steps), D(1 + 2 * steps), D(1 + 2 * steps), D(3),
            D(3), D(3), D(3, nz - 1), D(3, nz - 1), D(S1), D(S1), D(S2), D(S2), D(3), D(3),
        ],
        compiler_params=pltpu.CompilerParams(
            collective_id=0, has_side_effects=True, vmem_limit_bytes=56 * 1024 * 1024
        ),
    )(sets_one, sets_two, top, panel_one, panel_two, parent, pivot_one, pivot_two)


def solution(mesh):
    spec = P("prow", "pcol")
    return jax.shard_map(
        on_device,
        mesh=mesh,
        in_specs=(spec,) * 6 + (P(), P()),
        out_specs=(spec,) * 5,
        check_vma=False,
    )
```

time: 163 us -> 139 us (0.85)
  the two profiles are of different devices: /device:TPU:15 before, /device:TPU:37 now
where the time goes in v2:
time: 139 us
  Pallas kernels  130 us (94%)
  local copies, waits for them, and re-layouts  8.51 us (6%)
    pallas_call x1, Pallas kernels, on_device(): pl.pallas_call(functools.partial(kernel, cfg), out_shape=(out(share1, B),...  130 us
    unnamed x16, local copies, waits for them, and re-layouts  5.08 us
    reshape x2, local copies, waits for them, and re-layouts, on_device(): top.reshape(nbr, nr, sub, nbc, H, LN).transpose(0, 3, 1, 2, 4, 5)  3.43 us

profile of v2, /device:TPU:37, one launch (start us, length us, event | category | flops | bytes accessed | tf_op | source)
XLA Modules:
  0.0 139.1 jit_solution(6114915203990626219)
XLA Ops:
  0.6 1.9 %reshape.16 = f32[2,16,16,2,2,128]{5,4,3,2,1,0:T(2,128)S(1)} reshape(f32[512,512]{1,0:T(8,128)} %param.8) | data formatting | bytes 2097152 | tf_op jit(solution)/shard_map/reshape | solution.py:456
  2.5 0.0 copy-start.4
  2.5 1.6 %copy.13 = f32[2,16,16,2,2,128]{5,4,2,1,3,0:T(2,128)} copy(f32[2,16,16,2,2,128]{5,4,3,2,1,0:T(2,128)S(1)} %reshape.16) | data formatting | bytes 2097152 | tf_op jit(solution)/shard_map/reshape | solution.py:456
  4.1 0.0 copy-done.4
  4.1 0.7 copy.14.sets_two
  4.8 129.9 %shard_map.119 = (f32[160,256]{1,0:T(8,128)}, f32[16,256]{1,0:T(8,128)}, f32[80,512]{1,0:T(8,128)}, f32[16,512]{1,0:T(8,128)}, f32[16,512]{1,0:T(8,128)}) custom-call(s32[16,10]{1,0:T(8,128)} %sets_one.1, s32[32,5]{1,0:T(8,128)} %copy.14.sets_two, f32[4,16,16,2,128]{4,3,2,1,0:T(2,128)} %bitcast.3, f32[160,256]{1,0:T(8,128)} %panel_one.1, ...), custom_call_target="tpu_custom_call" | custom-call | tf_op jit(solution)/shard_map/pallas_call | solution.py:462
  134.7 0.0 copy-start.3
  134.7 0.0 copy-start
  134.7 1.6 %copy.20 = f32[160,256]{1,0:T(8,128)} copy(f32[160,256]{1,0:T(8,128)} %get-tuple-element.10) | data formatting | bytes 327680
  136.4 0.0 copy-done.3
  136.4 0.6 copy.21
  137.0 0.0 copy-done
  137.0 0.0 copy-start.2
  137.0 0.7 copy.22
  137.7 0.1 copy-done.2
  137.7 0.0 copy-start.1
  137.7 0.6 copy.23
  138.4 0.2 copy-done.1
  138.5 0.6 copy.24
Async XLA Ops:
  2.5 1.6 %copy-start.4 = (s32[32,5]{0,1:T(8,128)S(1)}, s32[32,5]{0,1:T(8,128)}, u32[]{:S(2)}) copy-start(s32[32,5]{0,1:T(8,128)} %param.15) | copy-start | bytes 1924
  134.7 1.7 %copy-start.3 = (f32[16,256]{1,0:T(8,128)S(1)}, f32[16,256]{1,0:T(8,128)}, u32[]{:S(2)}) copy-start(f32[16,256]{1,0:T(8,128)} %get-tuple-element.11) | copy-start | bytes 49156
  134.7 2.3 %copy-start = (f32[80,512]{1,0:T(8,128)S(1)}, f32[80,512]{1,0:T(8,128)}, u32[]{:S(2)}) copy-start(f32[80,512]{1,0:T(8,128)} %get-tuple-element.12) | copy-start | bytes 491524
  137.0 0.8 copy-start.2
  137.7 0.8 copy-start.1

commit v3 on v2

v3 whole, which is shorter than its diff:
```python
import functools

import jax
import jax.numpy as jnp
from jax import lax
from jax.experimental import pallas as pl
from jax.experimental.pallas import tpu as pltpu
from jax.sharding import PartitionSpec as P

MESH = pl.DeviceIdType.MESH
EXACT = lax.Precision.HIGHEST
F32 = jnp.float32
DIMS = (4, 4, 4, 2, 2)


def mm(a, b):
    return jnp.dot(a, b, precision=EXACT, preferred_element_type=F32)


def mm_t(a, b):
    return lax.dot_general(
        a, b, (((0,), (0,)), ((), ())), precision=EXACT, preferred_element_type=F32
    )


def kernel(
    cfg,
    sets_one, sets_two, top, panel_one, panel_two, parent, pivot_one, pivot_two,
    out1_in, out2_in, fin_in,
    arows, zs, packed, landed, grid, bundle, lg, l1, l2, pf,
    acc1, acc2, low1, low2, dir2, upper, b2s, part, sibpart, comb, sums, out1, out2, fin,
    swap_sem, a_send, a_recv, b_send, b_recv, c_send, c_recv,
    ring_send, ring_recv, sib_send, sib_recv, own_sem,
    x_send, x_recv, s_send, s_recv, o1_send, o1_recv, o2_send, o2_recv, back_send, back_recv,
):
    B, S1, S2 = cfg
    nx, ny, nzh, nzl, nk = DIMS
    nz = nzh * nzl
    nr = nz * nk
    nc = nx * ny
    sub = B // nr
    H = max(B // 128, 1)
    LN = B // H
    npc = S1 * S1 * H
    share1 = S1 * sub
    share2 = S2 * sub
    gathered = share1 + 2 * share2 + 2 * sub
    half = gathered // 2
    nq = top.shape[0]
    prow = lax.axis_index("prow")
    pcol = lax.axis_index("pcol")
    div, rem = lax.div, lax.rem
    zh, y = div(prow, ny), rem(prow, ny)
    zl, x, core = div(pcol, nx * nk), rem(div(pcol, nk), nx), rem(pcol, nk)
    z = zh * nzl + zl
    line = x * ny + y
    spot = z * nk + core
    y_hi, y_lo = div(y, nk), rem(y, nk)
    turn = y_lo if nzl == 2 else y_lo * 0

    def flip(a, b):
        return a + b - 2 * a * b

    def virtual(zz):
        return zz + turn * (1 - 2 * rem(zz, 2)) if nzl == 2 else zz

    zeta = virtual(z)
    me = zeta * nk + core

    def device(x, y, z, core):
        return (div(z, nzl) * ny + y, rem(z, nzl) * (nx * nk) + x * nk + core)

    def to_member(m):
        return device(x, y, virtual(div(m, nk)), rem(m, nk))

    def to_spot(m):
        return device(x, y, div(m, nk), rem(m, nk))

    def share_of(zz, k):
        return virtual(zz) * nk + k

    def node_of(dx, dy):
        return div(dy, nk) * (nx * nk) + dx * nk + rem(dy, nk)

    taker = device(x, zl * nk + core, zh * nzl + (flip(y_hi, core) if nzl == 2 else y_hi), y_lo)
    holder = device(x, (flip(zl, y_lo) if nzl == 2 else zl) * nk + core, zh * nzl + y_hi, y_lo)
    apart = lax.min(lax.abs(y - (zl * nk + core)) + (core if nzl == 2 else core * 0), 1)
    away = apart == 1
    sibling = device(x, y, z, 1 - core)

    if nx == 4 and ny == 4:
        near = [(1, 0), (3, 0), (0, 1), (0, 3), (1, 1), (3, 3), (1, 3), (3, 1),
                (2, 0), (0, 2), (2, 1), (2, 3), (1, 2), (3, 2), (2, 2)]
    else:
        near = [(i, j) for i in range(nx) for j in range(ny) if i + j > 0]

    def shift(k):
        dx = near[k][0] + core * (near[nc - 2 - k][0] - near[k][0])
        dy = near[k][1] + core * (near[nc - 2 - k][1] - near[k][1])
        return rem(x + dx, nx), rem(y + dy, ny), dx * ny + dy

    def each(n, f):
        def body(k, _):
            f(k)
            return 0
        lax.fori_loop(0, n, body, 0)

    def rcopy(src, dst, ss, rs, dev):
        return pltpu.make_async_remote_copy(
            src_ref=src, dst_ref=dst, send_sem=ss, recv_sem=rs, device_id=dev, device_id_type=MESH
        )

    barrier = pltpu.get_barrier_semaphore()

    def greet(dev):
        pl.semaphore_signal(barrier, inc=1, device_id=dev, device_id_type=MESH)

    for dz in range(nz):
        for dk in range(nk):
            if dz + dk > 0:
                greet(device(x, y, rem(z + dz, nz), rem(core + dk, nk)))
    for dx, dy in near:
        greet(device(rem(x + dx, nx), rem(y + dy, ny), z, core))

    @pl.when(away)
    def _():
        greet(taker)
        greet(holder)

    bundle[0:share1, :] = panel_one[...]
    at = share1
    for ch in range(2):
        bundle[at : at + share2, :] = panel_two[:, ch * B : (ch + 1) * B]
        at += share2
    for ch in range(2):
        bundle[at : at + sub, :] = parent[:, ch * B : (ch + 1) * B]
        at += sub
    bundle[at : at + sub, :] = pivot_one[...]
    at += sub
    for ch in range(2):
        bundle[at : at + sub, :] = pivot_two[:, ch * B : (ch + 1) * B]
        at += sub

    pl.semaphore_wait(barrier, nr + nc - 2 + 2 * apart)

    swap = rcopy(bundle, lg.at[prow], swap_sem.at[0], swap_sem.at[1], taker)

    @pl.when(away)
    def _():
        swap.start()

    def a_copy(k):
        d = rem(spot + k + 1, nr)
        return rcopy(top.at[:, d], arows.at[pl.ds(spot * nq, nq)], a_send.at[k], a_recv.at[k], to_spot(d))

    each(nr - 1, lambda k: a_copy(k).start())
    own_a = pltpu.make_async_copy(top.at[:, spot], arows.at[pl.ds(spot * nq, nq)], own_sem.at[0])
    own_a.start()

    steps = nz // 2
    STREAMS = [(1, 0), (-1, 1), (1, 1), (-1, 0)]

    def length(way, piece):
        return steps if (way == 1) == (piece == 0) else steps - 1

    def ring_copy(way, piece, s):
        to = rem(z + way + nz, nz)
        owner = share_of(rem(z - way * s + nz, nz), core)
        ref = lg.at[owner, pl.ds(piece * half, half)]
        w = 0 if way == 1 else 1
        return rcopy(ref, ref, ring_send.at[w, piece, s], ring_recv.at[w, piece, s], device(x, y, to, core))

    def sib_copy(way, piece, s):
        owner = share_of(rem(z - way * s + nz, nz), core)
        ref = lg.at[owner, pl.ds(piece * half, half)]
        w = 0 if way == 1 else 1
        return rcopy(ref, ref, sib_send.at[w, piece, s], sib_recv.at[w, piece, s], sibling)

    def pass_on(s):
        for way, piece in STREAMS:
            n = length(way, piece)
            if s <= n:
                ring_copy(way, piece, s - 1).wait_recv()
                if s < n:
                    ring_copy(way, piece, s).start()
                sib_copy(way, piece, s).start()

    own_a.wait()
    each(nr - 1, lambda k: a_copy(k).wait_recv())

    nb = nr * nq

    def b_copy(k):
        dx, dy, n = shift(k)
        return rcopy(
            arows.at[:, dx * ny + dy], zs.at[pl.ds(line * nb, nb)], b_send.at[n], b_recv.at[n], device(dx, dy, z, core)
        )

    for k in range(nc - 1):
        b_copy(k).start()
    own_b = pltpu.make_async_copy(arows.at[:, line], zs.at[pl.ds(line * nb, nb)], own_sem.at[1])
    own_b.start()

    @pl.when(away)
    def _():
        swap.wait_recv()

    @pl.when(jnp.logical_not(away))
    def _():
        lg[prow] = bundle[...]

    for way, piece in STREAMS:
        if length(way, piece) > 0:
            ring_copy(way, piece, 0).start()
    for piece in range(2):
        sib_copy(1, piece, 0).start()

    pass_on(1)

    own_b.wait()
    for k in range(nc - 1):
        b_copy(k).wait_recv()

    nbr = 2
    nbc = nq // nbr

    def pack(dx, dy):
        d = dx * ny + dy
        j = node_of(dx, dy)
        cols = []
        for s in range(S1):
            q = sets_one[j, s]
            c = div(q, nbc)
            cc = div(c, nk)
            cols.append(rem(cc, nx) * (ny * nb) + div(cc, nx) * (nk * nq) + rem(c, nk) * nq + rem(q, nbc))

        def row(a):
            p = sets_one[j, a]
            r = div(p, nbr)
            at = rem(r, ny) * nb + div(r, ny) * (nzl * nk * nq) + rem(p, nbr) * nbc
            for b in range(S1):
                packed[d, pl.ds((a * S1 + b) * H, H), :] = zs[at + cols[b]]

        each(S1, row)

    def c_copy(k):
        dx, dy, n = shift(k)
        return rcopy(
            packed.at[dx * ny + dy], landed.at[pl.ds(line * npc, npc)], c_send.at[n], c_recv.at[n],
            device(dx, dy, z, core),
        )

    for k in range(nc - 1):
        pack(*shift(k)[:2])
        c_copy(k).start()
    pack(x, y)
    own_c = pltpu.make_async_copy(packed.at[line], landed.at[pl.ds(line * npc, npc)], own_sem.at[2])
    own_c.start()

    for s in range(2, steps + 1):
        pass_on(s)

    for piece in range(2):
        sib_copy(1, piece, 0).wait_recv()
    for s in range(1, steps + 1):
        for way, piece in STREAMS:
            if s <= length(way, piece):
                sib_copy(way, piece, s).wait_recv()

    def spread(m):
        l1[pl.ds(m * share1, share1), :] = lg[m, 0:share1, :]
        for ch in range(2):
            o = share1 + ch * share2
            l2[ch, pl.ds(m * share2, share2), :] = lg[m, o : o + share2, :]
            o = share1 + 2 * share2 + ch * sub
            pf[ch, pl.ds(m * sub, sub), :] = lg[m, o : o + sub, :]

    each(nr, spread)

    own_c.wait()
    for k in range(nc - 1):
        c_copy(k).wait_recv()

    def assemble(b):
        for a in range(S1):
            for h in range(H):
                i = (a * S1 + b) * H + h
                grid[b, a * sub : (a + 1) * sub, h * LN : (h + 1) * LN] = landed[pl.ds(i, nc, stride=npc), :]

    each(S1, assemble)

    acc1[...] = jnp.zeros_like(acc1)

    def step_one(b):
        acc1[...] -= mm(grid[b], l1[pl.ds(pl.multiple_of(b * B, B), B), :]).reshape(acc1.shape)

    each(S1, step_one)

    def o1_copy(a):
        g = a * nr + spot
        return div(g, S1), rcopy(
            acc1.at[a], out1.at[pl.ds((rem(g, S1)) * sub, sub)],
            o1_send.at[a], o1_recv.at[rem(g, S1)], to_member(div(g, S1)),
        )

    def o2_copy(t):
        g = t * nr + spot
        return div(g, S2), rcopy(
            b2s.at[t], out2.at[pl.ds((rem(g, S2)) * sub, sub)],
            o2_send.at[t], o2_recv.at[rem(g, S2)], to_member(div(g, S2)),
        )

    def send_out(n, copy, src, dst):
        def go(a):
            d, cp = copy(a)

            @pl.when(d != me)
            def _():
                cp.start()

            @pl.when(d == me)
            def _():
                at = rem(a * nr + spot, n) * sub
                dst[pl.ds(pl.multiple_of(at, sub), sub), :] = src[a]

        each(n, go)

    def take_out(n, src, dst, send, recv):
        def go(a):
            s = rem(me * n + a, nr)

            @pl.when(s != spot)
            def _():
                rcopy(src.at[0], dst.at[pl.ds(a * sub, sub)], send.at[a], recv.at[a], to_spot(s)).wait_recv()

        each(n, go)

    def done_out(n, copy):
        def go(a):
            d, cp = copy(a)

            @pl.when(d != me)
            def _():
                cp.wait_send()

        each(n, go)

    send_out(S1, o1_copy, acc1, out1)

    def x_copy(g, cs):
        return rcopy(part.at[:, 1 - core, :, cs], sibpart.at[:, :, cs], x_send.at[g], x_recv.at[g], sibling)

    def s_copy(g, cs, k):
        d = rem(zeta + k + 1, nz)
        return rcopy(
            comb.at[d, :, cs], sums.at[zeta, :, cs], s_send.at[g, k], s_recv.at[g, k], device(x, y, virtual(d), core)
        )

    spans = [pl.ds(0, B), pl.ds(B, 2 * B), pl.ds(3 * B, 2 * B)]

    def combine(g):
        cs = spans[g]
        x_copy(g, cs).wait_recv()
        comb[:, :, cs] = part[:, core, :, cs] + sibpart[:, :, cs]
        for k in range(nz - 1):
            s_copy(g, cs, k).start()

    node = node_of(x, y)
    for a in range(S1):
        low1[a * sub : (a + 1) * sub, :] = l1[pl.ds(pl.multiple_of(a * B + spot * sub, sub), sub), :]
    square = mm_t(low1[...], acc1[...].reshape(S1 * sub, B))
    part[:, :, :, 0:B] = square.reshape(nz, nk, sub, B)
    x_copy(0, spans[0]).start()
    pivot1 = lg[me, gathered : gathered + sub, :]

    for ch in range(2):
        for t in range(S2):
            low2[t * sub : (t + 1) * sub, :] = l2[ch, pl.ds(pl.multiple_of(t * B + spot * sub, sub), sub), :]
        pos = []
        for t in range(S2):
            want = sets_two[2 * node + ch, t]
            at = 0
            for s in range(S1):
                at = at + s * (1 - lax.min(lax.abs(sets_one[node, s] - want), 1))
            pos.append(lax.min(at, S1 - 1))
        acc2[...] = jnp.zeros_like(acc2)
        for t in range(S2):
            acc2[...] += mm(grid[pos[t]], l2[ch, t * B : (t + 1) * B, :]).reshape(acc2.shape)
        for t in range(S2):
            dir2[t * sub : (t + 1) * sub, :] = acc2[pos[t]]
            upper[t * sub : (t + 1) * sub, :] = acc1[pos[t]]
        pc = pf[ch]
        u = upper[...]
        l2c = low2[...]
        b2 = -(dir2[...] + mm(u, pc))
        b2s[:, :, ch * B : (ch + 1) * B] = b2.reshape(S2, sub, B)
        cross = mm_t(u, l2c)
        inner = cross - mm(part[:, :, :, 0:B].reshape(B, B), pc)
        mine = pf[ch, pl.ds(pl.multiple_of(me * sub, sub), sub), :]
        last = mm_t(pc, inner) - mm_t(l2c, b2) + mm_t(mine, mm(pivot1, pc))
        o = B + 2 * ch * B
        part[:, :, :, o : o + B] = cross.reshape(nz, nk, sub, B)
        part[:, :, :, o + B : o + 2 * B] = last.reshape(nz, nk, sub, B)
        x_copy(ch + 1, spans[ch + 1]).start()
        combine(ch)

    send_out(S2, o2_copy, b2s, out2)
    combine(2)

    take_out(S1, acc1, out1, o1_send, o1_recv)
    take_out(S2, b2s, out2, o2_send, o2_recv)
    backs = [
        rcopy(out1, out1_in, back_send.at[0], back_recv.at[0], holder),
        rcopy(out2, out2_in, back_send.at[1], back_recv.at[1], holder),
        rcopy(fin, fin_in, back_send.at[2], back_recv.at[2], holder),
    ]

    @pl.when(away)
    def _():
        backs[0].start()
        backs[1].start()

    for g in range(3):
        for k in range(nz - 1):
            s_copy(g, spans[g], k).wait_recv()

    total = comb[zeta]
    for k in range(1, nz):
        total = total + sums[rem(zeta + k, nz)]
    corner = pivot1 - total[:, 0:B]
    fin[:, 0:B] = corner
    for ch in range(2):
        o = B + 2 * ch * B
        p2 = gathered + sub + ch * sub
        fin[:, (1 + ch) * B : (2 + ch) * B] = -(mm(corner, pf[ch]) + total[:, o : o + B])
        fin[:, (3 + ch) * B : (4 + ch) * B] = lg[me, p2 : p2 + sub, :] + total[:, o + B : o + 2 * B]

    @pl.when(away)
    def _():
        backs[2].start()
        for cp in backs:
            cp.wait_recv()

    @pl.when(jnp.logical_not(away))
    def _():
        out1_in[...] = out1[...]
        out2_in[...] = out2[...]
        fin_in[...] = fin[...]

    @pl.when(away)
    def _():
        swap.wait_send()
        for cp in backs:
            cp.wait_send()

    each(nr - 1, lambda k: a_copy(k).wait_send())
    for k in range(nc - 1):
        b_copy(k).wait_send()
        c_copy(k).wait_send()
    for way, piece in STREAMS:
        for s in range(length(way, piece)):
            ring_copy(way, piece, s).wait_send()
            sib_copy(way, piece, s + 1).wait_send()
    for piece in range(2):
        sib_copy(1, piece, 0).wait_send()
    for g in range(3):
        x_copy(g, spans[g]).wait_send()
        for k in range(nz - 1):
            s_copy(g, spans[g], k).wait_send()
    done_out(S1, o1_copy)
    done_out(S2, o2_copy)


def deliver(one, two, rest, below_one, corner_one, below_two, beside, corner_two):
    B = one.shape[1]
    below_one[...] = one[...]
    below_two[...] = two[...]
    corner_one[...] = rest[:, 0:B]
    beside[...] = rest[:, B : 3 * B]
    corner_two[...] = rest[:, 3 * B : 5 * B]


def on_device(top, panel_one, panel_two, parent, pivot_one, pivot_two, sets_one, sets_two):
    nx, ny, nzh, nzl, nk = DIMS
    nz = nzh * nzl
    nr = nz * nk
    nc = nx * ny
    S1 = sets_one.shape[1]
    S2 = sets_two.shape[1]
    B = panel_one.shape[1]
    sub = B // nr
    H = max(B // 128, 1)
    LN = B // H
    nbr, nbc = top.shape[0] // B, top.shape[1] // B
    nq = nbr * nbc
    npc = S1 * S1 * H
    share1, share2 = S1 * sub, S2 * sub
    gathered = share1 + 2 * share2 + 2 * sub
    whole = gathered + 3 * sub
    steps = nz // 2
    cfg = (B, S1, S2)
    top = top.reshape(nbr, nr, sub, nbc, H, LN).transpose(0, 3, 1, 2, 4, 5).reshape(nq, nr, sub, H, LN)
    vmem = pl.BlockSpec(memory_space=pltpu.VMEM)
    smem = pl.BlockSpec(memory_space=pltpu.SMEM)
    V = lambda *s: pltpu.VMEM(s, F32)
    D = lambda *s: pltpu.SemaphoreType.DMA(s)
    out = lambda *s: jax.ShapeDtypeStruct(s, F32)
    one, two, rest = pl.pallas_call(
        functools.partial(kernel, cfg),
        out_shape=(out(share1, B), out(share2, 2 * B), out(sub, 5 * B)),
        in_specs=[smem, smem] + [vmem] * 6,
        out_specs=(vmem,) * 3,
        scratch_shapes=[
            V(nr * nq, sub, H, LN),
            V(nc * nr * nq, H, LN),
            V(nc, npc, LN),
            V(nc * npc, LN),
            V(S1, share1, B),
            V(whole, B),
            V(nr, whole, B),
            V(S1 * B, B),
            V(2, S2 * B, B),
            V(2, B, B),
            V(S1, sub, B),
            V(S1, sub, B),
            V(share1, B),
            V(share2, B),
            V(share2, B),
            V(share2, B),
            V(S2, sub, 2 * B),
            V(nz, nk, sub, 5 * B),
            V(nz, sub, 5 * B),
            V(nz, sub, 5 * B),
            V(nz, sub, 5 * B),
            V(share1, B),
            V(share2, 2 * B),
            V(sub, 5 * B),
            D(2),
            D(nr - 1), D(nr - 1), D(nc), D(nc), D(nc), D(nc),
            D(2, 2, steps), D(2, 2, steps), D(2, 2, steps + 1), D(2, 2, steps + 1), D(3),
            D(3), D(3), D(3, nz - 1), D(3, nz - 1), D(S1), D(S1), D(S2), D(S2), D(3), D(3),
        ],
        compiler_params=pltpu.CompilerParams(
            collective_id=0, has_side_effects=True, vmem_limit_bytes=56 * 1024 * 1024
        ),
    )(sets_one, sets_two, top, panel_one, panel_two, parent, pivot_one, pivot_two)
    return pl.pallas_call(
        deliver,
        out_shape=(out(share1, B), out(sub, B), out(share2, 2 * B), out(sub, 2 * B), out(sub, 2 * B)),
        in_specs=[vmem] * 3,
        out_specs=(vmem,) * 5,
    )(one, two, rest)


def solution(mesh):
    spec = P("prow", "pcol")
    return jax.shard_map(
        on_device,
        mesh=mesh,
        in_specs=(spec,) * 6 + (P(), P()),
        out_specs=(spec,) * 5,
        check_vma=False,
    )
```

time: 139 us -> 123 us (0.88)
  the two profiles are of different devices: /device:TPU:37 before, /device:TPU:1 now
where the time goes in v3:
time: 123 us; the launch traced here: 122 us
  Pallas kernels  117 us (95%)
  local copies, waits for them, and re-layouts  4.13 us (3%)
    pallas_call x1, Pallas kernels, on_device(): pl.pallas_call(functools.partial(kernel, cfg), out_shape=(out(share1, B),...  115 us
    reshape x2, local copies, waits for them, and re-layouts, on_device(): top.reshape(nbr, nr, sub, nbc, H, LN).transpose(0, 3, 1, 2, 4, 5)  3.43 us

profile of v3, /device:TPU:1, one launch (start us, length us, event | category | flops | bytes accessed | tf_op | source)
XLA Modules:
  0.0 121.7 jit_solution(8782530249612668696)
XLA Ops:
  0.6 1.9 %reshape.16 = f32[2,16,16,2,2,128]{5,4,3,2,1,0:T(2,128)S(1)} reshape(f32[512,512]{1,0:T(8,128)} %param.8) | data formatting | bytes 2097152 | tf_op jit(solution)/shard_map/reshape | solution.py:502
  2.5 0.0 copy-start
  2.5 1.6 %copy.13 = f32[2,16,16,2,2,128]{5,4,2,1,3,0:T(2,128)} copy(f32[2,16,16,2,2,128]{5,4,3,2,1,0:T(2,128)S(1)} %reshape.16) | data formatting | bytes 2097152 | tf_op jit(solution)/shard_map/reshape | solution.py:502
  4.1 0.0 copy-done
  4.1 0.7 copy.14.sets_two
  4.8 115.1 %shard_map.119 = (f32[160,256]{1,0:T(8,128)}, f32[80,512]{1,0:T(8,128)}, f32[16,1280]{1,0:T(8,128)}) custom-call(s32[16,10]{1,0:T(8,128)} %sets_one.1, s32[32,5]{1,0:T(8,128)} %copy.14.sets_two, f32[4,16,16,2,128]{4,3,2,1,0:T(2,128)} %bitcast.3, f32[160,256]{1,0:T(8,128)} %panel_one.1, f32[80,512]{1,0:T(8,128)} %panel_two.1, f32[16,512]{1,0:T(8,128)} %parent.1, ...), custom_call_target="tpu_custom_call" | custom-call | tf_op jit(solution)/shard_map/pallas_call | solution.py:508
  119.9 1.8 %shard_map.120 = (f32[160,256]{1,0:T(8,128)}, f32[16,256]{1,0:T(8,128)}, f32[80,512]{1,0:T(8,128)}, f32[16,512]{1,0:T(8,128)}, f32[16,512]{1,0:T(8,128)}) custom-call(f32[160,256]{1,0:T(8,128)} %get-tuple-element.8.one, f32[80,512]{1,0:T(8,128)} %get-tuple-element.9.two, f32[16,1280]{1,0:T(8,128)} %get-tuple-element.10.rest), custom_call_target="tpu_custom_call" | custom-call | tf_op jit(solution)/shard_map/pallas_call | solution.py:547
Async XLA Ops:
  2.5 1.6 %copy-start = (s32[32,5]{0,1:T(8,128)S(1)}, s32[32,5]{0,1:T(8,128)}, u32[]{:S(2)}) copy-start(s32[32,5]{0,1:T(8,128)} %param.15) | copy-start | bytes 1924

commit v4 on v3

--- a/solution.py
+++ b/solution.py
@@ -28,10 +28,10 @@
     sets_one, sets_two, top, panel_one, panel_two, parent, pivot_one, pivot_two,
     out1_in, out2_in, fin_in,
     arows, zs, packed, landed, grid, bundle, lg, l1, l2, pf,
-    acc1, acc2, low1, low2, dir2, upper, b2s, part, sibpart, comb, sums, out1, out2, fin,
+    acc1, acc2, low1, low2, dir2, upper, b2s, part, sibpart, comb, sums, fin,
     swap_sem, a_send, a_recv, b_send, b_recv, c_send, c_recv,
     ring_send, ring_recv, sib_send, sib_recv, own_sem,
-    x_send, x_recv, s_send, s_recv, o1_send, o1_recv, o2_send, o2_recv, back_send, back_recv,
+    x_send, x_recv, s_send, s_recv, o1_send, o1_recv, o2_send, o2_recv, back_sem,
 ):
     B, S1, S2 = cfg
     nx, ny, nzh, nzl, nk = DIMS
@@ -46,7 +46,7 @@
     share2 = S2 * sub
     gathered = share1 + 2 * share2 + 2 * sub
     half = gathered // 2
-    nq = top.shape[0]
+    nbr, nbc = top.shape[0], top.shape[3]
     prow = lax.axis_index("prow")
     pcol = lax.axis_index("pcol")
     div, rem = lax.div, lax.rem
@@ -84,7 +84,9 @@
 
     taker = device(x, zl * nk + core, zh * nzl + (flip(y_hi, core) if nzl == 2 else y_hi), y_lo)
     holder = device(x, (flip(zl, y_lo) if nzl == 2 else zl) * nk + core, zh * nzl + y_hi, y_lo)
-    apart = lax.min(lax.abs(y - (zl * nk + core)) + (core if nzl == 2 else core * 0), 1)
+    home = zl * nk + core
+    abroad = lax.min(lax.abs(y - home), 1)
+    apart = lax.min(abroad + (core if nzl == 2 else core * 0), 1)
     away = apart == 1
     sibling = device(x, y, z, 1 - core)
 
@@ -122,9 +124,18 @@
     for dx, dy in near:
         greet(device(rem(x + dx, nx), rem(y + dy, ny), z, core))
 
+    for dz in range(nz):
+        for dk in range(nk):
+            dev = device(x, home, rem(z + dz, nz), rem(core + dk, nk))
+            if dz + dk > 0:
+                greet(dev)
+            else:
+                @pl.when(abroad == 1)
+                def _():
+                    greet(dev)
+
     @pl.when(away)
     def _():
-        greet(taker)
         greet(holder)
 
     bundle[0:share1, :] = panel_one[...]
@@ -141,20 +152,23 @@
         bundle[at : at + sub, :] = pivot_two[:, ch * B : (ch + 1) * B]
         at += sub
 
-    pl.semaphore_wait(barrier, nr + nc - 2 + 2 * apart)
-
-    swap = rcopy(bundle, lg.at[prow], swap_sem.at[0], swap_sem.at[1], taker)
+    pl.semaphore_wait(barrier, 2 * nr + nc - 3 + abroad + apart)
+
+    def swap_copy(piece):
+        rows = pl.ds(0, half) if piece == 0 else pl.ds(half, gathered + 3 * sub - half)
+        return rcopy(bundle.at[rows], lg.at[prow, rows], swap_sem.at[0, piece], swap_sem.at[1, piece], taker)
 
     @pl.when(away)
     def _():
-        swap.start()
+        for piece in range(2):
+            swap_copy(piece).start()
 
     def a_copy(k):
         d = rem(spot + k + 1, nr)
-        return rcopy(top.at[:, d], arows.at[pl.ds(spot * nq, nq)], a_send.at[k], a_recv.at[k], to_spot(d))
+        return rcopy(top.at[:, d], arows.at[pl.ds(spot * nbr, nbr)], a_send.at[k], a_recv.at[k], to_spot(d))
 
     each(nr - 1, lambda k: a_copy(k).start())
-    own_a = pltpu.make_async_copy(top.at[:, spot], arows.at[pl.ds(spot * nq, nq)], own_sem.at[0])
+    own_a = pltpu.make_async_copy(top.at[:, spot], arows.at[pl.ds(spot * nbr, nbr)], own_sem.at[0])
     own_a.start()
 
     steps = nz // 2
@@ -188,7 +202,7 @@
     own_a.wait()
     each(nr - 1, lambda k: a_copy(k).wait_recv())
 
-    nb = nr * nq
+    nb = nr * nbr
 
     def b_copy(k):
         dx, dy, n = shift(k)
@@ -201,18 +215,18 @@
     own_b = pltpu.make_async_copy(arows.at[:, line], zs.at[pl.ds(line * nb, nb)], own_sem.at[1])
     own_b.start()
 
-    @pl.when(away)
-    def _():
-        swap.wait_recv()
-
     @pl.when(jnp.logical_not(away))
     def _():
         lg[prow] = bundle[...]
 
-    for way, piece in STREAMS:
-        if length(way, piece) > 0:
-            ring_copy(way, piece, 0).start()
     for piece in range(2):
+        @pl.when(away)
+        def _():
+            swap_copy(piece).wait_recv()
+
+        for way, part_of in STREAMS:
+            if part_of == piece and length(way, piece) > 0:
+                ring_copy(way, piece, 0).start()
         sib_copy(1, piece, 0).start()
 
     pass_on(1)
@@ -220,9 +234,6 @@
     own_b.wait()
     for k in range(nc - 1):
         b_copy(k).wait_recv()
-
-    nbr = 2
-    nbc = nq // nbr
 
     def pack(dx, dy):
         d = dx * ny + dy
@@ -232,14 +243,14 @@
             q = sets_one[j, s]
             c = div(q, nbc)
             cc = div(c, nk)
-            cols.append(rem(cc, nx) * (ny * nb) + div(cc, nx) * (nk * nq) + rem(c, nk) * nq + rem(q, nbc))
+            cols.append((rem(cc, nx) * (ny * nb) + div(cc, nx) * (nk * nbr) + rem(c, nk) * nbr, rem(q, nbc)))
 
         def row(a):
             p = sets_one[j, a]
             r = div(p, nbr)
-            at = rem(r, ny) * nb + div(r, ny) * (nzl * nk * nq) + rem(p, nbr) * nbc
+            at = rem(r, ny) * nb + div(r, ny) * (nzl * nk * nbr) + rem(p, nbr)
             for b in range(S1):
-                packed[d, pl.ds((a * S1 + b) * H, H), :] = zs[at + cols[b]]
+                packed[d, pl.ds((a * S1 + b) * H, H), :] = zs[at + cols[b][0], cols[b][1]]
 
         each(S1, row)
 
@@ -296,29 +307,35 @@
 
     each(S1, step_one)
 
+    def holder_of(m):
+        return device(x, rem(m, ny), div(m, ny) * nzl + y_hi, y_lo)
+
     def o1_copy(a):
         g = a * nr + spot
         return div(g, S1), rcopy(
-            acc1.at[a], out1.at[pl.ds((rem(g, S1)) * sub, sub)],
-            o1_send.at[a], o1_recv.at[rem(g, S1)], to_member(div(g, S1)),
+            acc1.at[a], out1_in.at[pl.ds(rem(g, S1) * sub, sub)],
+            o1_send.at[a], o1_recv.at[rem(g, S1)], holder_of(div(g, S1)),
         )
 
     def o2_copy(t):
         g = t * nr + spot
         return div(g, S2), rcopy(
-            b2s.at[t], out2.at[pl.ds((rem(g, S2)) * sub, sub)],
-            o2_send.at[t], o2_recv.at[rem(g, S2)], to_member(div(g, S2)),
+            b2s.at[t], out2_in.at[pl.ds(rem(g, S2) * sub, sub)],
+            o2_send.at[t], o2_recv.at[rem(g, S2)], holder_of(div(g, S2)),
         )
+
+    def stays(d):
+        return lax.min(lax.abs(d - prow) + abroad, 1) == 0
 
     def send_out(n, copy, src, dst):
         def go(a):
             d, cp = copy(a)
 
-            @pl.when(d != me)
+            @pl.when(jnp.logical_not(stays(d)))
             def _():
                 cp.start()
 
-            @pl.when(d == me)
+            @pl.when(stays(d))
             def _():
                 at = rem(a * nr + spot, n) * sub
                 dst[pl.ds(pl.multiple_of(at, sub), sub), :] = src[a]
@@ -327,11 +344,14 @@
 
     def take_out(n, src, dst, send, recv):
         def go(a):
-            s = rem(me * n + a, nr)
-
-            @pl.when(s != spot)
+            m = rem(prow * n + a, nr)
+
+            @pl.when(lax.min(lax.abs(m - spot) + abroad, 1) == 1)
             def _():
-                rcopy(src.at[0], dst.at[pl.ds(a * sub, sub)], send.at[a], recv.at[a], to_spot(s)).wait_recv()
+                rcopy(
+                    src.at[0], dst.at[pl.ds(a * sub, sub)], send.at[a], recv.at[a],
+                    device(x, home, div(m, nk), rem(m, nk)),
+                ).wait_recv()
 
         each(n, go)
 
@@ -339,13 +359,13 @@
         def go(a):
             d, cp = copy(a)
 
-            @pl.when(d != me)
+            @pl.when(jnp.logical_not(stays(d)))
             def _():
                 cp.wait_send()
 
         each(n, go)
 
-    send_out(S1, o1_copy, acc1, out1)
+    send_out(S1, o1_copy, acc1, out1_in)
 
     def x_copy(g, cs):
         return rcopy(part.at[:, 1 - core, :, cs], sibpart.at[:, :, cs], x_send.at[g], x_recv.at[g], sibling)
@@ -404,21 +424,8 @@
         x_copy(ch + 1, spans[ch + 1]).start()
         combine(ch)
 
-    send_out(S2, o2_copy, b2s, out2)
     combine(2)
-
-    take_out(S1, acc1, out1, o1_send, o1_recv)
-    take_out(S2, b2s, out2, o2_send, o2_recv)
-    backs = [
-        rcopy(out1, out1_in, back_send.at[0], back_recv.at[0], holder),
-        rcopy(out2, out2_in, back_send.at[1], back_recv.at[1], holder),
-        rcopy(fin, fin_in, back_send.at[2], back_recv.at[2], holder),
-    ]
-
-    @pl.when(away)
-    def _():
-        backs[0].start()
-        backs[1].start()
+    send_out(S2, o2_copy, b2s, out2_in)
 
     for g in range(3):
         for k in range(nz - 1):
@@ -435,23 +442,28 @@
         fin[:, (1 + ch) * B : (2 + ch) * B] = -(mm(corner, pf[ch]) + total[:, o : o + B])
         fin[:, (3 + ch) * B : (4 + ch) * B] = lg[me, p2 : p2 + sub, :] + total[:, o + B : o + 2 * B]
 
+    back = rcopy(fin, fin_in, back_sem.at[0], back_sem.at[1], holder)
+
     @pl.when(away)
     def _():
-        backs[2].start()
-        for cp in backs:
-            cp.wait_recv()
+        back.start()
+
+    take_out(S1, acc1, out1_in, o1_send, o1_recv)
+    take_out(S2, b2s, out2_in, o2_send, o2_recv)
+
+    @pl.when(away)
+    def _():
+        back.wait_recv()
 
     @pl.when(jnp.logical_not(away))
     def _():
-        out1_in[...] = out1[...]
-        out2_in[...] = out2[...]
         fin_in[...] = fin[...]
 
     @pl.when(away)
     def _():
-        swap.wait_send()
-        for cp in backs:
-            cp.wait_send()
+        for piece in range(2):
+            swap_copy(piece).wait_send()
+        back.wait_send()
 
     each(nr - 1, lambda k: a_copy(k).wait_send())
     for k in range(nc - 1):
@@ -492,14 +504,13 @@
     H = max(B // 128, 1)
     LN = B // H
     nbr, nbc = top.shape[0] // B, top.shape[1] // B
-    nq = nbr * nbc
     npc = S1 * S1 * H
     share1, share2 = S1 * sub, S2 * sub
     gathered = share1 + 2 * share2 + 2 * sub
     whole = gathered + 3 * sub
     steps = nz // 2
     cfg = (B, S1, S2)
-    top = top.reshape(nbr, nr, sub, nbc, H, LN).transpose(0, 3, 1, 2, 4, 5).reshape(nq, nr, sub, H, LN)
+    top = top.reshape(nbr, nr, sub, nbc, H, LN)
     vmem = pl.BlockSpec(memory_space=pltpu.VMEM)
     smem = pl.BlockSpec(memory_space=pltpu.SMEM)
     V = lambda *s: pltpu.VMEM(s, F32)
@@ -511,8 +522,8 @@
         in_specs=[smem, smem] + [vmem] * 6,
         out_specs=(vmem,) * 3,
         scratch_shapes=[
-            V(nr * nq, sub, H, LN),
-            V(nc * nr * nq, H, LN),
+            V(nr * nbr, sub, nbc, H, LN),
+            V(nc * nr * nbr, nbc, H, LN),
             V(nc, npc, LN),
             V(nc * npc, LN),
             V(S1, share1, B),
@@ -532,13 +543,11 @@
             V(nz, sub, 5 * B),
             V(nz, sub, 5 * B),
             V(nz, sub, 5 * B),
-            V(share1, B),
-            V(share2, 2 * B),
             V(sub, 5 * B),
-            D(2),
+            D(2, 2),
             D(nr - 1), D(nr - 1), D(nc), D(nc), D(nc), D(nc),
             D(2, 2, steps), D(2, 2, steps), D(2, 2, steps + 1), D(2, 2, steps + 1), D(3),
-            D(3), D(3), D(3, nz - 1), D(3, nz - 1), D(S1), D(S1), D(S2), D(S2), D(3), D(3),
+            D(3), D(3), D(3, nz - 1), D(3, nz - 1), D(S1), D(S1), D(S2), D(S2), D(2),
         ],
         compiler_params=pltpu.CompilerParams(
             collective_id=0, has_side_effects=True, vmem_limit_bytes=56 * 1024 * 1024

time: 123 us -> 118 us (0.959); the launches traced: 122 us -> 118 us
  Pallas kernels: 117 us -> 113 us
    pallas_call x1, Pallas kernels: 115 us -> 111 us  [on_device(): pl.pallas_call(functools.partial(kernel, cfg), out_shape=(out(share1, B),...]
    reshape x2 -> x1, local copies, waits for them, and re-layouts: 3.43 us -> 2.86 us  [on_device(): top = top.reshape(nbr, nr, sub, nbc, H, LN)]
where the time goes in v4:
time: 118 us
  Pallas kernels  113 us (96%)
  local copies, waits for them, and re-layouts  4.23 us (4%)
    pallas_call x1, Pallas kernels, on_device(): pl.pallas_call(functools.partial(kernel, cfg), out_shape=(out(share1, B),...  111 us
    reshape x1, local copies, waits for them, and re-layouts, on_device(): top = top.reshape(nbr, nr, sub, nbc, H, LN)  2.86 us

profile of v4, /device:TPU:1, one launch (start us, length us, event | category | flops | bytes accessed | tf_op | source)
XLA Modules:
  0.0 118.0 jit_solution(6840194255182909760)
XLA Ops:
  0.6 1.4 %copy.13.sets_two = s32[32,5]{1,0:T(8,128)} copy(s32[32,5]{0,1:T(8,128)} %param.15) | data formatting | bytes 1280 | tf_op args[7]
  2.0 2.9 %reshape.13.top = f32[2,16,16,2,2,128]{5,4,3,2,1,0:T(2,128)} reshape(f32[512,512]{1,0:T(8,128)} %param.8) | data formatting | bytes 2097152 | tf_op jit(solution)/shard_map/reshape | solution.py:513
  4.9 111.4 %shard_map.119 = (f32[160,256]{1,0:T(8,128)}, f32[80,512]{1,0:T(8,128)}, f32[16,1280]{1,0:T(8,128)}) custom-call(s32[16,10]{1,0:T(8,128)} %sets_one.1, s32[32,5]{1,0:T(8,128)} %copy.13.sets_two, f32[2,16,16,2,2,128]{5,4,3,2,1,0:T(2,128)} %reshape.13.top, f32[160,256]{1,0:T(8,128)} %panel_one.1, f32[80,512]{1,0:T(8,128)} %panel_two.1, f32[16,512]{1,0:T(8,128)} %parent.1, ...), custom_call_target="tpu_custom_call" | custom-call | tf_op jit(solution)/shard_map/pallas_call | solution.py:519
  116.2 1.8 %shard_map.120 = (f32[160,256]{1,0:T(8,128)}, f32[16,256]{1,0:T(8,128)}, f32[80,512]{1,0:T(8,128)}, f32[16,512]{1,0:T(8,128)}, f32[16,512]{1,0:T(8,128)}) custom-call(f32[160,256]{1,0:T(8,128)} %get-tuple-element.8.one, f32[80,512]{1,0:T(8,128)} %get-tuple-element.9.two, f32[16,1280]{1,0:T(8,128)} %get-tuple-element.10.rest), custom_call_target="tpu_custom_call" | custom-call | tf_op jit(solution)/shard_map/pallas_call | solution.py:556

commit v5 on v4

--- a/solution.py
+++ b/solution.py
@@ -163,12 +163,15 @@
         for piece in range(2):
             swap_copy(piece).start()
 
-    def a_copy(k):
+    def a_copy(k, part_of):
         d = rem(spot + k + 1, nr)
-        return rcopy(top.at[:, d], arows.at[pl.ds(spot * nbr, nbr)], a_send.at[k], a_recv.at[k], to_spot(d))
-
-    each(nr - 1, lambda k: a_copy(k).start())
-    own_a = pltpu.make_async_copy(top.at[:, spot], arows.at[pl.ds(spot * nbr, nbr)], own_sem.at[0])
+        return rcopy(
+            top.at[part_of, d], arows.at[part_of, spot], a_send.at[part_of, k], a_recv.at[part_of, k], to_spot(d)
+        )
+
+    for i in range(nbr):
+        each(nr - 1, lambda k: a_copy(k, i).start())
+    own_a = pltpu.make_async_copy(top.at[:, spot], arows.at[:, spot], own_sem.at[0])
     own_a.start()
 
     steps = nz // 2
@@ -200,20 +203,27 @@
                 sib_copy(way, piece, s).start()
 
     own_a.wait()
-    each(nr - 1, lambda k: a_copy(k).wait_recv())
 
     nb = nr * nbr
 
-    def b_copy(k):
+    def b_copy(k, part_of):
         dx, dy, n = shift(k)
         return rcopy(
-            arows.at[:, dx * ny + dy], zs.at[pl.ds(line * nb, nb)], b_send.at[n], b_recv.at[n], device(dx, dy, z, core)
-        )
-
-    for k in range(nc - 1):
-        b_copy(k).start()
-    own_b = pltpu.make_async_copy(arows.at[:, line], zs.at[pl.ds(line * nb, nb)], own_sem.at[1])
-    own_b.start()
+            arows.at[part_of, :, dx * ny + dy], zs.at[pl.ds((line * nbr + part_of) * nr, nr)],
+            b_send.at[part_of, n], b_recv.at[part_of, n], device(dx, dy, z, core),
+        )
+
+    own_b = [
+        pltpu.make_async_copy(
+            arows.at[i, :, line], zs.at[pl.ds((line * nbr + i) * nr, nr)], own_sem.at[1 + i]
+        )
+        for i in range(nbr)
+    ]
+    for i in range(nbr):
+        each(nr - 1, lambda k: a_copy(k, i).wait_recv())
+        for k in range(nc - 1):
+            b_copy(k, i).start()
+        own_b[i].start()
 
     @pl.when(jnp.logical_not(away))
     def _():
@@ -231,9 +241,10 @@
 
     pass_on(1)
 
-    own_b.wait()
-    for k in range(nc - 1):
-        b_copy(k).wait_recv()
+    for i in range(nbr):
+        own_b[i].wait()
+        for k in range(nc - 1):
+            b_copy(k, i).wait_recv()
 
     def pack(dx, dy):
         d = dx * ny + dy
@@ -243,12 +254,12 @@
             q = sets_one[j, s]
             c = div(q, nbc)
             cc = div(c, nk)
-            cols.append((rem(cc, nx) * (ny * nb) + div(cc, nx) * (nk * nbr) + rem(c, nk) * nbr, rem(q, nbc)))
+            cols.append((rem(cc, nx) * (ny * nb) + div(cc, nx) * nk + rem(c, nk), rem(q, nbc)))
 
         def row(a):
             p = sets_one[j, a]
             r = div(p, nbr)
-            at = rem(r, ny) * nb + div(r, ny) * (nzl * nk * nbr) + rem(p, nbr)
+            at = rem(r, ny) * nb + rem(p, nbr) * nr + div(r, ny) * (nzl * nk)
             for b in range(S1):
                 packed[d, pl.ds((a * S1 + b) * H, H), :] = zs[at + cols[b][0], cols[b][1]]
 
@@ -265,7 +276,7 @@
         pack(*shift(k)[:2])
         c_copy(k).start()
     pack(x, y)
-    own_c = pltpu.make_async_copy(packed.at[line], landed.at[pl.ds(line * npc, npc)], own_sem.at[2])
+    own_c = pltpu.make_async_copy(packed.at[line], landed.at[pl.ds(line * npc, npc)], own_sem.at[1 + nbr])
     own_c.start()
 
     for s in range(2, steps + 1):
@@ -465,9 +476,11 @@
             swap_copy(piece).wait_send()
         back.wait_send()
 
-    each(nr - 1, lambda k: a_copy(k).wait_send())
+    for i in range(nbr):
+        each(nr - 1, lambda k: a_copy(k, i).wait_send())
+        for k in range(nc - 1):
+            b_copy(k, i).wait_send()
     for k in range(nc - 1):
-        b_copy(k).wait_send()
         c_copy(k).wait_send()
     for way, piece in STREAMS:
         for s in range(length(way, piece)):
@@ -522,7 +535,7 @@
         in_specs=[smem, smem] + [vmem] * 6,
         out_specs=(vmem,) * 3,
         scratch_shapes=[
-            V(nr * nbr, sub, nbc, H, LN),
+            V(nbr, nr, sub, nbc, H, LN),
             V(nc * nr * nbr, nbc, H, LN),
             V(nc, npc, LN),
             V(nc * npc, LN),
@@ -545,8 +558,8 @@
             V(nz, sub, 5 * B),
             V(sub, 5 * B),
             D(2, 2),
-            D(nr - 1), D(nr - 1), D(nc), D(nc), D(nc), D(nc),
-            D(2, 2, steps), D(2, 2, steps), D(2, 2, steps + 1), D(2, 2, steps + 1), D(3),
+            D(nbr, nr - 1), D(nbr, nr - 1), D(nbr, nc), D(nbr, nc), D(nc), D(nc),
+            D(2, 2, steps), D(2, 2, steps), D(2, 2, steps + 1), D(2, 2, steps + 1), D(2 + nbr),
             D(3), D(3), D(3, nz - 1), D(3, nz - 1), D(S1), D(S1), D(S2), D(S2), D(2),
         ],
         compiler_params=pltpu.CompilerParams(

time: 118 us -> 117 us (level)
  no operation moved by 1% of the time
where the time goes in v5:
time: 117 us
  Pallas kernels  112 us (96%)
  local copies, waits for them, and re-layouts  4.23 us (4%)
    pallas_call x1, Pallas kernels, on_device(): pl.pallas_call(functools.partial(kernel, cfg), out_shape=(out(share1, B),...  110 us
    reshape x1, local copies, waits for them, and re-layouts, on_device(): top = top.reshape(nbr, nr, sub, nbc, H, LN)  2.86 us

profile of v5, /device:TPU:1, one launch (start us, length us, event | category | flops | bytes accessed | tf_op | source)
XLA Modules:
  0.0 117.1 jit_solution(472752160137931105)
XLA Ops:
  0.6 1.4 %copy.13.sets_two = s32[32,5]{1,0:T(8,128)} copy(s32[32,5]{0,1:T(8,128)} %param.15) | data formatting | bytes 1280 | tf_op args[7]
  2.0 2.9 %reshape.13.top = f32[2,16,16,2,2,128]{5,4,3,2,1,0:T(2,128)} reshape(f32[512,512]{1,0:T(8,128)} %param.8) | data formatting | bytes 2097152 | tf_op jit(solution)/shard_map/reshape | solution.py:526
  4.9 110.5 %shard_map.119 = (f32[160,256]{1,0:T(8,128)}, f32[80,512]{1,0:T(8,128)}, f32[16,1280]{1,0:T(8,128)}) custom-call(s32[16,10]{1,0:T(8,128)} %sets_one.1, s32[32,5]{1,0:T(8,128)} %copy.13.sets_two, f32[2,16,16,2,2,128]{5,4,3,2,1,0:T(2,128)} %reshape.13.top, f32[160,256]{1,0:T(8,128)} %panel_one.1, f32[80,512]{1,0:T(8,128)} %panel_two.1, f32[16,512]{1,0:T(8,128)} %parent.1, ...), custom_call_target="tpu_custom_call" | custom-call | tf_op jit(solution)/shard_map/pallas_call | solution.py:532
  115.3 1.8 %shard_map.120 = (f32[160,256]{1,0:T(8,128)}, f32[16,256]{1,0:T(8,128)}, f32[80,512]{1,0:T(8,128)}, f32[16,512]{1,0:T(8,128)}, f32[16,512]{1,0:T(8,128)}) custom-call(f32[160,256]{1,0:T(8,128)} %get-tuple-element.8.one, f32[80,512]{1,0:T(8,128)} %get-tuple-element.9.two, f32[16,1280]{1,0:T(8,128)} %get-tuple-element.10.rest), custom_call_target="tpu_custom_call" | custom-call | tf_op jit(solution)/shard_map/pallas_call | solution.py:569

commit v6 on v5

--- a/solution.py
+++ b/solution.py
@@ -311,12 +311,10 @@
 
     each(S1, assemble)
 
-    acc1[...] = jnp.zeros_like(acc1)
-
-    def step_one(b):
-        acc1[...] -= mm(grid[b], l1[pl.ds(pl.multiple_of(b * B, B), B), :]).reshape(acc1.shape)
-
-    each(S1, step_one)
+    total = mm(grid[0], l1[0:B, :])
+    for b in range(1, S1):
+        total = total + mm(grid[b], l1[b * B : (b + 1) * B, :])
+    acc1[...] = -total.reshape(acc1.shape)
 
     def holder_of(m):
         return device(x, rem(m, ny), div(m, ny) * nzl + y_hi, y_lo)
@@ -414,9 +412,10 @@
             for s in range(S1):
                 at = at + s * (1 - lax.min(lax.abs(sets_one[node, s] - want), 1))
             pos.append(lax.min(at, S1 - 1))
-        acc2[...] = jnp.zeros_like(acc2)
-        for t in range(S2):
-            acc2[...] += mm(grid[pos[t]], l2[ch, t * B : (t + 1) * B, :]).reshape(acc2.shape)
+        total = mm(grid[pos[0]], l2[ch, 0:B, :])
+        for t in range(1, S2):
+            total = total + mm(grid[pos[t]], l2[ch, t * B : (t + 1) * B, :])
+        acc2[...] = total.reshape(acc2.shape)
         for t in range(S2):
             dir2[t * sub : (t + 1) * sub, :] = acc2[pos[t]]
             upper[t * sub : (t + 1) * sub, :] = acc1[pos[t]]

time: 117 us -> 116 us (level)
  no operation moved by 1% of the time
where the time goes in v6:
time: 116 us
  Pallas kernels  111 us (96%)
  local copies, waits for them, and re-layouts  4.23 us (4%)
    pallas_call x1, Pallas kernels, on_device(): pl.pallas_call(functools.partial(kernel, cfg), out_shape=(out(share1, B),...  109 us
    reshape x1, local copies, waits for them, and re-layouts, on_device(): top = top.reshape(nbr, nr, sub, nbc, H, LN)  2.86 us

profile of v6, /device:TPU:1, one launch (start us, length us, event | category | flops | bytes accessed | tf_op | source)
XLA Modules:
  0.0 116.1 jit_solution(4290300405809855552)
XLA Ops:
  0.6 1.4 %copy.13.sets_two = s32[32,5]{1,0:T(8,128)} copy(s32[32,5]{0,1:T(8,128)} %param.15) | data formatting | bytes 1280 | tf_op args[7]
  2.0 2.9 %reshape.13.top = f32[2,16,16,2,2,128]{5,4,3,2,1,0:T(2,128)} reshape(f32[512,512]{1,0:T(8,128)} %param.8) | data formatting | bytes 2097152 | tf_op jit(solution)/shard_map/reshape | solution.py:525
  4.9 109.5 %shard_map.119 = (f32[160,256]{1,0:T(8,128)}, f32[80,512]{1,0:T(8,128)}, f32[16,1280]{1,0:T(8,128)}) custom-call(s32[16,10]{1,0:T(8,128)} %sets_one.1, s32[32,5]{1,0:T(8,128)} %copy.13.sets_two, f32[2,16,16,2,2,128]{5,4,3,2,1,0:T(2,128)} %reshape.13.top, f32[160,256]{1,0:T(8,128)} %panel_one.1, f32[80,512]{1,0:T(8,128)} %panel_two.1, f32[16,512]{1,0:T(8,128)} %parent.1, ...), custom_call_target="tpu_custom_call" | custom-call | tf_op jit(solution)/shard_map/pallas_call | solution.py:531
  114.3 1.8 %shard_map.120 = (f32[160,256]{1,0:T(8,128)}, f32[16,256]{1,0:T(8,128)}, f32[80,512]{1,0:T(8,128)}, f32[16,512]{1,0:T(8,128)}, f32[16,512]{1,0:T(8,128)}) custom-call(f32[160,256]{1,0:T(8,128)} %get-tuple-element.8.one, f32[80,512]{1,0:T(8,128)} %get-tuple-element.9.two, f32[16,1280]{1,0:T(8,128)} %get-tuple-element.10.rest), custom_call_target="tpu_custom_call" | custom-call | tf_op jit(solution)/shard_map/pallas_call | solution.py:568
